TPU v7x, 128 devices: a whole 4x4x4 slice. The times are simulated.
128 devices in a mesh: ka: 16 (over z_lo, x, core), band: 8 (over z_hi, y).
Axes of the slice: x: 4, y: 4, z: 4 (z_hi: 2, z_lo: 2; z = z_hi * 2 + z_lo), core: 2. Of those that a mesh axis runs over, the one named last changes fastest.
Arguments:
- orbitals: float32 [16, 64, 2, 4096], P('ka', 'band'), may hold values from -6 to 6
- point_index: int32 [2048], replicated, may hold values from 0 to 4095, as said below
- kernel: bfloat16 [2048, 2048], replicated
- q_weight: float32 [16, 2048], replicated, may hold values from 0.5 to 2
- q_table: int32 [16, 16], replicated, may hold values from 0 to 15
- occ_count: int32 [16], replicated, may hold values from 16 to 64
Outputs:
- exchange: float32 [16, 64, 2, 2048], P(None, 'band', None, 'ka')
Inputs may be any that keep to these rules, and one draw needn't show every extreme that they name: point_index[j] is 2 j or 2 j + 1.
All inputs are finite; a program needn't handle non-finite values.
Results may differ from a plain program's by a relative error of at most 0.00049.
Values sent between devices are 32-bit elements; how exact they have to be, the bound alone decides.
No kernel may reach another device: no remote copies, remote signals or barrier semaphores. Data moves between devices by JAX's collectives and lax.ppermute only.
A program may use at most 64 MiB of HBM per device.

v0:
```python
import jax
import jax.numpy as jnp
from jax import lax
from jax.sharding import PartitionSpec as P

STEPS = 3


def shifted(value, axis, by):
    size = lax.axis_size(axis)
    return lax.ppermute(value, axis, [(i, (i + by) % size) for i in range(size)])


def contribution(mine, other, weight, live, kernel):
    ar = other[:, 0]
    ai = other[:, 1]
    br = mine[:, 0]
    bi = mine[:, 1]
    real_part = br[:, None] * ar[None] + bi[:, None] * ai[None]
    imag_part = ar[None] * bi[:, None] - ai[None] * br[:, None]
    pair = (jnp.stack([real_part, imag_part], axis=2) * weight).astype(jnp.bfloat16)
    width = pair.shape[3]
    flat = pair.reshape(-1, width)
    screened = (
        jnp.dot(flat, kernel, preferred_element_type=jnp.float32).reshape(pair.shape) * weight
    )
    wr = screened[:, :, 0]
    wi = screened[:, :, 1]
    alive = live[None, :, None]
    term_re = jnp.sum(alive * (ar[None] * wr - ai[None] * wi), axis=1)
    term_im = jnp.sum(alive * (ar[None] * wi + ai[None] * wr), axis=1)
    return jnp.stack([term_re, term_im], axis=1)


def body(orbitals, point_index, kernel, q_weight, q_table, occ_count):
    mine = jnp.take(orbitals[0], point_index, axis=2)
    cycle_size = lax.axis_size("ka")
    kidx = lax.axis_index("ka")
    total_bands = mine.shape[0] * lax.axis_size("band")
    band_ids = jnp.arange(total_bands, dtype=jnp.int32)
    factor = -1.0 / jnp.sqrt(jnp.float32(STEPS * total_bands))
    total = jnp.zeros(mine.shape, jnp.float32)
    held = lax.all_gather(mine, "band", axis=0, tiled=True)
    for offset in range(STEPS):
        if offset > 0:
            held = shifted(held, "ka", 1)
        qidx = (kidx - offset) % cycle_size
        tidx = q_table[kidx, qidx]
        weight = lax.dynamic_index_in_dim(q_weight, tidx, 0, keepdims=False)
        live = (band_ids < occ_count[qidx]).astype(jnp.float32)
        total = total + contribution(mine, held, weight, live, kernel)
    result = total * factor
    return lax.all_to_all(result[None], "ka", split_axis=3, concat_axis=0, tiled=True)


def solution(mesh):
    placed = (P("ka", "band", None, None), P(), P(), P(), P(), P())
    return jax.shard_map(
        body, mesh=mesh, in_specs=placed, out_specs=P(None, "band", None, "ka"), check_vma=False
    )
```

profile of v0, /device:TPU:0, one launch (start us, length us, event | category | flops | bytes accessed | tf_op | source)
XLA Modules:
  0.0 203.9 jit_solution(12601322497418242800)
XLA Ops:
  6.5 0.0 all-gather.2.cloned.1.call-start
  6.5 0.7 fusion.26
  7.2 0.7 compare_and_fusion
  7.9 5.4 %copy.50 = f32[1,8,2,4096]{1,2,3,0:T(2,128)} copy(f32[1,8,2,4096]{3,2,1,0:T(2,128)} %param.6) | data formatting | bytes 524288 | tf_op args[0]
  13.3 16.6 %gather_fusion = f32[2048,8,2]{1,2,0:T(2,128)} fusion(f32[8,2,4096]{0,1,2:T(2,128)} %bitcast.101, s32[2048]{0:T(1024)S(1)} %fusion.26), kind=kCustom, calls=%fused_computation | custom fusion | bytes 270336 | tf_op jit(solution)/shard_map/jit(_take)/gather | solution.py:36
  30.0 10.0 %select_bitcast_fusion = f32[8,2,2048]{0,1,2:T(2,128)S(1)} fusion(f32[2048,8,2]{1,2,0:T(2,128)} %gather_fusion, pred[2048]{0:T(1024)(128)(4,1)S(1)} %compare_and_fusion), kind=kLoop, calls=%fused_computation.37 | loop fusion | flops 32768 | bytes 264192 | tf_op jit(solution)/shard_map/jit(_take)/select_n | solution.py:36
  39.9 1.9 copy.51
  41.8 0.0 all-gather.2.cloned.1.call-update
  41.8 0.0 copy-start.1
  41.8 50.0 %all-gather.2.cloned.1.call-done = f32[64,2,2048]{2,1,0:T(2,128)} async-done(((f32[8,2,2048]{2,1,0:T(2,128)}), f32[64,2,2048]{2,1,0:T(2,128)}) %all-gather.2.cloned.1.call-update) | async-done | bytes 1048592 | tf_op jit(solution)/shard_map/all_gather | solution.py:43
  91.9 0.0 copy-start
  91.9 2.9 %copy.55 = f32[64,2,2048]{2,0,1:T(8,128)} copy(f32[64,2,2048]{2,1,0:T(2,128)} %all-gather.2.cloned.1.call-done) | data formatting | bytes 2097152 | tf_op jit(solution)/shard_map/all_gather | solution.py:43
  94.8 0.0 collective-permute-start
  94.8 1.5 fusion.32
  100.1 2.7 %fusion.30 = (f32[8,1,2048]{0,1,2:T(1,128)}, f32[8,1,2048]{0,1,2:T(1,128)}) fusion(f32[8,2,2048]{0,1,2:T(2,128)S(1)} %select_bitcast_fusion), kind=kLoop, calls=%fused_computation.59 | loop fusion | bytes 262144 | tf_op jit(solution)/shard_map/slice | solution.py:17
  102.8 1.5 copy.52
  104.3 1.5 copy.53
  107.7 0.0 copy-done.1
  107.7 0.6 fusion.33
  108.4 0.6 compare_convert_fusion
  109.0 0.6 compare_convert_fusion.1
  109.6 1.0 constant_dynamic-slice_fusion
  110.6 0.8 collective-permute-done
  111.4 1.0 collective-permute-start.1
  112.5 0.5 compare_convert_fusion.2
  113.0 0.0 copy-done
  113.0 0.8 fusion.31
  113.8 0.2 copy.69
  114.0 1.3 slice_bitcast_fusion.9
  115.3 12.7 %collective-permute-done.1 = f32[64,2,2048]{2,0,1:T(8,128)S(1)} collective-permute-done((f32[64,2,2048]{2,0,1:T(8,128)}, f32[64,2,2048]{2,0,1:T(8,128)S(1)}, u32[]{:S(2)}, u32[]{:S(2)}) %collective-permute-start.1) | collective-permute-done | bytes 1048608 | tf_op jit(solution)/shard_map/ppermute | solution.py:11
  128.0 0.2 slice_bitcast_fusion.7
  128.2 5.7 %multiply_add_fusion = (f32[8,64,1,2048]{3,1,2,0:T(8,128)}, f32[8,64,1,2048]{3,1,2,0:T(8,128)}, f32[8,64,1,2048]{3,1,2,0:T(8,128)S(1)}, f32[8,64,1,2048]{3,1,2,0...) fusion(f32[64,2048]{1,0:T(8,128)S(1)} %get-tuple-element.20, ...), kind=kLoop, calls=%fused_computation.26 | loop fusion | flops 18874368 | bytes 28442624 | tf_op jit(solution)/shard_map/add | solution.py:19
  134.0 13.7 %fusion.15 = f32[8,64,2,2048]{3,1,2,0:T(8,128)S(1)} fusion(bf16[2048,2048]{1,0:T(8,128)(2,1)} %param.8, f32[8,64,1,2048]{3,1,2,0:T(8,128)} %get-tuple-element.14, f32[8,64,1,2048]{3,1,2,0:T(8,128)} %get-tuple-element.13, f32[2048]{0:T(1024)S(1)} %bitcast.113), kind=kOutput, calls=%fused_computation.15 | convolution fusion | flops 8598323200 | bytes 25174016 | tf_op jit(solution)/shard_map/dot_general | solution.py:25
  147.7 1.9 multiply_reduce_fusion.1
  149.6 12.5 %fusion.12 = f32[8,64,2,2048]{3,1,2,0:T(8,128)S(1)} fusion(bf16[2048,2048]{1,0:T(8,128)(2,1)} %param.8, f32[8,64,1,2048]{3,1,2,0:T(8,128)S(1)} %get-tuple-element.28, f32[8,64,1,2048]{3,1,2,0:T(8,128)} %get-tuple-element.29, f32[2048]{0:T(1024)S(1)} %bitcast.112), kind=kOutput, calls=%fused_computation.14 | convolution fusion | flops 8598323200 | bytes 25174016 | tf_op jit(solution)/shard_map/dot_general | solution.py:25
  162.1 1.9 multiply_reduce_fusion.3
  164.0 11.4 %fusion.9 = f32[8,64,2,2048]{3,1,2,0:T(8,128)S(1)} fusion(bf16[2048,2048]{1,0:T(8,128)(2,1)} %param.8, f32[8,64,1,2048]{3,1,2,0:T(8,128)S(1)} %get-tuple-element.30, f32[8,64,1,2048]{3,1,2,0:T(8,128)S(1)} %get-tuple-element.31, f32[2048]{0:T(1024)S(1)} %bitcast.111), kind=kOutput, calls=%fused_computation.13 | convolution fusion | flops 8598323200 | bytes 25174016 | tf_op jit(solution)/shard_map/dot_general | solution.py:25
  175.4 1.9 multiply_reduce_fusion.5
  177.4 1.0 copy.58
  178.4 3.3 %reshape.216 = f32[16,1,2048]{2,1,0:T(1,128)S(1)} reshape(f32[2048,1,2,8]{3,2,1,0:T(2,128)S(1)} %bitcast.97) | data formatting | bytes 262144
  181.7 9.0 %all_to_all.18 = f32[16,1,2048]{2,1,0:T(1,128)S(1)} all-to-all(f32[16,1,2048]{2,1,0:T(1,128)S(1)} %reshape.216), channel_id=1, replica_groups=mesh['ka'=16,'band'=8] {'ka'}, dimensions={0} | all-to-all | bytes 262144 | tf_op jit(solution)/shard_map/all_to_all | solution.py:53
  190.8 0.5 broadcast.217
  191.3 0.9 reduce
  192.2 3.2 %reshape.217 = f32[2048,1,2,8]{3,2,1,0:T(2,128)S(1)} reshape(f32[16,2048]{1,0:T(8,128)S(1)} %reduce) | data formatting | bytes 262144
  195.4 0.9 copy.59
  196.3 0.7 copy.60
  (1 shorter events, 0.0 us)
Async XLA Ops:
  6.5 85.3 %all-gather.2.cloned.1.call-start = ((), (), s32[]{:S(2)}) async-start(), calls=%async_computation.1 | async-start | bytes 1179648 | tf_op jit(solution)/shard_map/all_gather | solution.py:43
  41.8 65.9 %copy-start.1 = (s32[16]{0:T(128)S(1)}, s32[16]{0:T(128)}, u32[]{:S(2)}) copy-start(s32[16]{0:T(128)} %param.11) | copy-start | bytes 196
  91.9 21.1 %copy-start = (f32[64,2,2048]{2,1,0:T(2,128)S(1)}, f32[64,2,2048]{2,1,0:T(2,128)}, u32[]{:S(2)}) copy-start(f32[64,2,2048]{2,1,0:T(2,128)} %all-gather.2.cloned.1.call-done) | copy-start | bytes 3145732
  94.8 16.6 %collective-permute-start = (f32[64,2,2048]{2,0,1:T(8,128)}, f32[64,2,2048]{2,0,1:T(8,128)}, u32[]{:S(2)}, u32[]{:S(2)}) collective-permute-start(f32[64,2,2048]{2,0,1:T(8,128)} %copy.55), channel_id=1, source_target_pairs={{0,8},{8,16},{16,24},{24,32},{32,40},{40,48},{48,56},{56,64},{64,7... | collective-permute-start | bytes 3145736 | tf_op jit(solution)/shard_map/ppermute | solution.py:11
  111.4 16.5 %collective-permute-start.1 = (f32[64,2,2048]{2,0,1:T(8,128)}, f32[64,2,2048]{2,0,1:T(8,128)S(1)}, u32[]{:S(2)}, u32[]{:S(2)}) collective-permute-start(f32[64,2,2048]{2,0,1:T(8,128)} %collective-permute-done), channel_id=1, source_target_pairs={{0,8},{8,16},{16,24},{24,32},{32,40},{40,48},{48,56},{56,64},{64,7... | collective-permute-start | bytes 3145736 | tf_op jit(solution)/shard_map/ppermute | solution.py:11
Sparse Core Ops, SparseCore 0:
  41.9 49.8 all-gather.1
where the time goes:
time: 206 us; the launch traced here: 204 us
  waiting for transfers between devices  63.6 us (31%)
  local copies, waits for them, and re-layouts  47.7 us (23%)
  matrix products  37.6 us (18%)
  other arithmetic  25.6 us (12%)
  between operations  19.3 us (9%)
  blocking collectives  9.04 us (4%)
    all_gather x1, waiting for transfers between devices, body(): held = lax.all_gather(mine, 'band', axis=0, tiled=True)  50 us
    dot_general x3, matrix products, contribution(): jnp.dot(flat, kernel, preferred_element_type=jnp.float32)  37.6 us
    gather x1, local copies, waits for them, and re-layouts, body(): mine = jnp.take(orbitals[0], point_index, axis=2)  16.6 us
    ppermute x2, waiting for transfers between devices, shifted(): lax.ppermute(value, axis, [(i, (i + by) % size) for i in range(size)])  13.5 us
    unnamed x8, local copies, waits for them, and re-layouts  12.1 us
    select_n x1, other arithmetic, body(): mine = jnp.take(orbitals[0], point_index, axis=2)  9.97 us
    all_to_all x1, blocking collectives, body(): lax.all_to_all(result[None], 'ka', split_axis=3, concat_axis=0, tiled=True)  9.04 us
    add x1, other arithmetic, contribution(): real_part = br[:, None] * ar[None] + bi[:, None] * ai[None]  5.75 us
  transfers between devices with their start and end apart: 3, of which 3 were waited for; matrix products, arithmetic and copies ran while one was open for 6% of the time, Pallas kernels for 0%

commit v1 on v0

v1 whole, which is shorter than its diff:
```python
import jax
import jax.numpy as jnp
from jax import lax
from jax.experimental import pallas as pl
from jax.experimental.pallas import tpu as pltpu
from jax.sharding import PartitionSpec as P

STEPS = 3
KPTS = 16
BLOCKS = 8
ROWS = 16
POINTS = 2048
HALF = POINTS // 2
TILE = 256
DEPTH = 128
FACTOR = -1.0 / (STEPS * 64) ** 0.5
F32, BF16 = jnp.float32, jnp.bfloat16


def device(i, c, zh, y):
    return ((i % 8) * 2 + c) * BLOCKS + zh * 4 + y % 4


def everyone():
    return [(i, c, zh, y) for i in range(8) for c in range(2) for zh in range(2) for y in range(4)]


def gather_pairs(tz, ty):
    pairs = []
    for i, c, zh, y in everyone():
        if y % 2 == c:
            to = device(i, c, zh ^ tz, y + 2 * ty)
        else:
            to = device(i, 1 - c, zh ^ tz, y + 1 + 2 * ty)
        pairs.append((device(i, c, zh, y), to))
    return pairs


def own_band_pairs():
    pairs = []
    for i, c, zh, y in everyone():
        stay = c == 0 and y % 2 == 1
        pairs.append((device(i, c, zh, y), device(i if stay else i + 1, c, zh, y)))
    return pairs


def next_band_pairs():
    pairs = []
    for i, c, zh, y in everyone():
        stay = c == 0 and y % 2 == 0
        pairs.append((device(i, c, zh, y), device(i if stay else i + 1, c, zh, y ^ 1)))
    return pairs


def core_pairs():
    return [(device(i, c, zh, y), device(i, 1 - c, zh, y)) for i, c, zh, y in everyone()]


def send(value, pairs):
    return lax.ppermute(value, ("ka", "band"), pairs)


def place():
    ka, band = lax.axis_index("ka"), lax.axis_index("band")
    return ka // 2, ka % 2, band // 4, band % 4, band


def pick_kernel(index_ref, orb_ref, out_ref):
    for j in range(POINTS // 128):
        idx = jnp.broadcast_to(index_ref[:, j * 128 : (j + 1) * 128], (8, 128)) & 127
        low = lax.broadcasted_iota(jnp.int32, (8, 128), 1) < 64
        for part in range(2):
            left = orb_ref[:, part, 2 * j * 128 : (2 * j + 1) * 128]
            right = orb_ref[:, part, (2 * j + 1) * 128 : (2 * j + 2) * 128]
            got = jnp.where(
                low,
                jnp.take_along_axis(left, idx, axis=1, mode="promise_in_bounds"),
                jnp.take_along_axis(right, idx, axis=1, mode="promise_in_bounds"),
            )
            out_ref[part * 8 : part * 8 + 8, j * 128 : (j + 1) * 128] = got


def pick(orbitals, point_index):
    return pl.pallas_call(
        pick_kernel,
        out_shape=jax.ShapeDtypeStruct((ROWS, POINTS), F32),
        name="pick_points",
    )(point_index.reshape(1, POINTS), orbitals)


def halves(value, c):
    out = []
    for j in range(value.shape[1] // 256):
        a, b = value[:, j * 256 : j * 256 + 128], value[:, j * 256 + 128 : j * 256 + 256]
        low = lax.broadcasted_iota(jnp.int32, a.shape, 1) < 64
        first = jnp.where(c == 0, a, pltpu.roll(a, 64, 1))
        second = jnp.where(c == 0, pltpu.roll(b, 64, 1), b)
        out.append(jnp.where(low, first, second))
    return jnp.concatenate(out, axis=1)


def columns_kernel(k_ref, out_ref):
    c = place()[1]
    out_ref[...] = halves(k_ref[...].astype(F32), c).astype(BF16)


def columns(kernel):
    rows = 256
    return pl.pallas_call(
        columns_kernel,
        grid=(POINTS // rows,),
        in_specs=[pl.BlockSpec((rows, POINTS), lambda r: (r, 0))],
        out_specs=pl.BlockSpec((rows, HALF), lambda r: (r, 0)),
        out_shape=jax.ShapeDtypeStruct((POINTS, HALF), BF16),
        cost_estimate=pl.CostEstimate(flops=POINTS * POINTS * 4, bytes_accessed=12 * 2**20, transcendentals=0),
        name="kernel_columns",
    )(kernel)


def split(value):
    high = value.astype(BF16)
    return high, (value - high.astype(F32)).astype(BF16)


def exchange_kernel(table_ref, occ_ref, weight_ref, k_ref, *refs):
    mine, theirs = refs[0:4], refs[4:8]
    before = refs[8:12]
    out_ref = refs[12]
    x_ref, xcat_ref, p_ref, pt_ref, f_ref, mhi_ref, mlo_ref = refs[13:]
    i, c, zh, y, band = place()
    parity = y % 2
    kpoint = 2 * i + parity
    same = c == parity
    own_step = jnp.where(same, 2, 1)
    steps = (0, own_step, 3 - own_step)
    points = [lax.rem(kpoint - s + KPTS, KPTS) for s in steps]

    @pl.when(pl.program_id(0) == 0)
    def _():
        for group, shift in ((mine, jnp.where(same, 0, 1)), (theirs, jnp.where(same, 1, 0))):
            for t, ref in enumerate(group):
                tz, ty = t // 2, t % 2
                block = jnp.where(zh == tz, 0, 4) + lax.rem(y - shift - 2 * ty + 8, 4)
                value = ref[...]
                x_ref[block] = value
                high, low = split(value)
                row = pl.multiple_of(block * ROWS, ROWS)
                xcat_ref[pl.ds(row, ROWS), :] = high
                xcat_ref[pl.ds(pl.multiple_of(128 + row, ROWS), ROWS), :] = low
        f_ref[...] = jnp.zeros_like(f_ref)
        for g in range(STEPS):
            f_ref[pl.ds(g, 1), :] = weight_ref[pl.ds(table_ref[kpoint, points[g]], 1), :]
        p_ref[96:, :] = jnp.zeros((DEPTH - 96, POINTS), F32)
        p_ref[0:16, :] = x_ref[band]
        p_ref[16:32, :] = x_ref[band ^ 1]
        for n in range(4):
            p_ref[32 + 16 * n : 48 + 16 * n, :] = before[n][...]
        for j in range(POINTS // 128):
            cols = slice(j * 128, (j + 1) * 128)
            scaled = jnp.concatenate(
                [p_ref[32 * g : 32 * g + 32, cols] * f_ref[g : g + 1, cols] for g in range(STEPS)] + [p_ref[96:, cols]], axis=0
            )
            high, low = split(scaled.T)
            pt_ref[cols, 0:128] = high
            pt_ref[cols, 128:256] = high
            pt_ref[cols, 256:384] = low

    start = pl.multiple_of(pl.program_id(0) * 2 * TILE, 2 * TILE)
    f_here = halves(f_ref[:, pl.ds(start, 2 * TILE)], c)
    row = lax.broadcasted_iota(jnp.int32, (32, TILE), 0)
    number = jnp.where(row < 16, band, band ^ 1) * 8 + (row & 7)
    plain, turned = [], []
    for g in range(STEPS):
        live = number < occ_ref[points[g]]
        value = halves(p_ref[32 * g : 32 * g + 32, pl.ds(start, 2 * TILE)], c) * f_here[g : g + 1]
        value = jnp.where(live, value, 0.0)
        plain.append(value)
        turned += [value[8:16], -value[0:8], value[24:32], -value[16:24]]
    fill = [jnp.zeros((DEPTH - 96, TILE), F32)]
    both = jnp.concatenate([jnp.concatenate(plain + fill, axis=0), jnp.concatenate(turned + fill, axis=0)], axis=1)
    high, low = split(both)
    w = jnp.concatenate([high, low, high], axis=0)
    chunk = 512
    for n in range(POINTS // chunk):
        rows = slice(n * chunk, (n + 1) * chunk)
        e = jnp.dot(pt_ref[rows, :], w, preferred_element_type=F32)
        kf = k_ref[rows, :].astype(F32)
        for part in range(2):
            cols = slice(part * TILE, (part + 1) * TILE)
            high, low = split(e[:, cols] * kf)
            mhi_ref[rows, cols] = high
            mlo_ref[rows, cols] = low
    first = jnp.dot(xcat_ref[...], mhi_ref[...], preferred_element_type=F32)
    second = jnp.dot(xcat_ref[0:128, :], mlo_ref[...], preferred_element_type=F32)
    r = first[0:128] + first[128:256] + second
    low_lanes = lax.broadcasted_iota(jnp.int32, (8, 128), 1) < 64
    for b in range(BLOCKS):
        top, bottom = r[b * ROWS : b * ROWS + 8], r[b * ROWS + 8 : b * ROWS + 16]
        re = top[:, :TILE] - bottom[:, TILE:]
        im = top[:, TILE:] + bottom[:, :TILE]
        for j in range(TILE // 128):
            a, d = re[:, j * 128 : (j + 1) * 128], im[:, j * 128 : (j + 1) * 128]
            out_ref[2 * j, b] = jnp.where(low_lanes, a, pltpu.roll(d, 64, 1))
            out_ref[2 * j + 1, b] = jnp.where(low_lanes, pltpu.roll(a, 64, 1), d)


def exchange(q_table, occ_count, q_weight, half_kernel, mine, theirs, before):
    whole = pl.BlockSpec(memory_space=pltpu.VMEM)
    smem = pl.BlockSpec(memory_space=pltpu.SMEM)
    return pl.pallas_call(
        exchange_kernel,
        grid=(HALF // TILE,),
        in_specs=[smem, smem, whole, pl.BlockSpec((POINTS, TILE), lambda u: (0, u))] + [whole] * 12,
        out_specs=pl.BlockSpec((4, BLOCKS, 8, 128), lambda u: (u, 0, 0, 0)),
        out_shape=jax.ShapeDtypeStruct((KPTS, BLOCKS, 8, 128), F32),
        scratch_shapes=[
            pltpu.VMEM((BLOCKS, ROWS, POINTS), F32),
            pltpu.VMEM((256, POINTS), BF16),
            pltpu.VMEM((DEPTH, POINTS), F32),
            pltpu.VMEM((POINTS, 3 * DEPTH), BF16),
            pltpu.VMEM((8, POINTS), F32),
            pltpu.VMEM((POINTS, 2 * TILE), BF16),
            pltpu.VMEM((POINTS, 2 * TILE), BF16),
        ],
        compiler_params=pltpu.CompilerParams(vmem_limit_bytes=40 * 2**20),
        cost_estimate=pl.CostEstimate(flops=14 * 10**9, bytes_accessed=8 * 2**20, transcendentals=0),
        name="exchange_terms",
    )(q_table, occ_count, q_weight, half_kernel, *mine, *theirs, *before)


def total_kernel(in_ref, out_ref):
    low = lax.broadcasted_iota(jnp.int32, (8, 128), 1) < 64
    for k in range(KPTS):
        i, parity = k // 2, k % 2
        sums = []
        for c in range(2):
            parts = [in_ref[device(i, c, zh, parity + 2 * h)] for zh in range(2) for h in range(2)]
            sums.append(((parts[0] + parts[1]) + (parts[2] + parts[3])) * FACTOR)
        out_ref[k, :, 0, :] = jnp.where(low, sums[0], pltpu.roll(sums[1], 64, 1))
        out_ref[k, :, 1, :] = jnp.where(low, pltpu.roll(sums[0], 64, 1), sums[1])


def total(parts):
    return pl.pallas_call(
        total_kernel,
        out_shape=jax.ShapeDtypeStruct((KPTS, 8, 2, 128), F32),
        name="total",
    )(parts)


def body(orbitals, point_index, kernel, q_weight, q_table, occ_count):
    block = pick(orbitals[0], point_index)
    mine = [send(block, gather_pairs(t // 2, t % 2)) for t in range(4)]
    before = [send(block, own_band_pairs()), send(block, next_band_pairs())]
    theirs = [send(value, core_pairs()) for value in mine]
    before_theirs = [send(value, core_pairs()) for value in before]
    half_kernel = columns(kernel)
    parts = exchange(q_table, occ_count, q_weight, half_kernel, mine, theirs, before + before_theirs)
    got = lax.all_to_all(parts.reshape(128, 8, 128), ("ka", "band"), 0, 0, tiled=True)
    return total(got)


def solution(mesh):
    placed = (P("ka", "band", None, None), P(), P(), P(), P(), P())
    return jax.shard_map(body, mesh=mesh, in_specs=placed, out_specs=P(None, "band", None, "ka"), check_vma=False)
```

time: 206 us -> 67.6 us (0.33)
  waiting for transfers between devices: 63.6 us -> 6.53 us
  local copies, waits for them, and re-layouts: 47.7 us -> 2.19 us
  matrix products: 37.6 us -> 0 us
  other arithmetic: 25.6 us -> 0 us
  Pallas kernels: 0 us -> 23.9 us
  between operations: 19.3 us -> 0.08 us
  starting transfers between devices: 1.03 us -> 15.1 us
  blocking collectives: 9.04 us -> 19.3 us
    all_gather x1 -> x0, waiting for transfers between devices: 50 us -> none  [body(): held = lax.all_gather(mine, 'band', axis=0, tiled=True)]
    dot_general x3 -> x0, matrix products: 37.6 us -> none  [contribution(): jnp.dot(flat, kernel, preferred_element_type=jnp.float32)]
    pallas_call x0 -> x4, Pallas kernels: none -> 23.9 us  [the longest x1 11.2 us: exchange(): pl.pallas_call(exchange_kernel, grid=(HALF // TILE,), in_specs=[smem, sme...]
    gather x1 -> x0, local copies, waits for them, and re-layouts: 16.6 us -> none  [body(): mine = jnp.take(orbitals[0], point_index, axis=2)]
    ppermute x2 -> x12, starting transfers between devices: 1.03 us -> 15.1 us  [send(): return lax.ppermute(value, ('ka', 'band'), pairs)]
    all_to_all x1, blocking collectives: 9.04 us -> 19.3 us  [body(): lax.all_to_all(parts.reshape(128, 8, 128), ('ka', 'band'), 0, 0, tiled=True)]
    select_n x1 -> x0, other arithmetic: 9.97 us -> none  [body(): mine = jnp.take(orbitals[0], point_index, axis=2)]
    unnamed x8, local copies, waits for them, and re-layouts: 12.1 us -> 2.19 us
  transfers between devices with their start and end apart: 3 -> 12, of which waited for: 3 -> 2; matrix products, arithmetic and copies ran while one was open for 6% -> 0% of each run, Pallas kernels for 0% -> 13%
where the time goes in v1:
time: 67.6 us; the launch traced here: 67.1 us
  Pallas kernels  23.9 us (35%)
  blocking collectives  19.3 us (29%)
  starting transfers between devices  15.1 us (22%)
  waiting for transfers between devices  6.53 us (10%)
  local copies, waits for them, and re-layouts  2.19 us (3%)
    all_to_all x1, blocking collectives, body(): lax.all_to_all(parts.reshape(128, 8, 128), ('ka', 'band'), 0, 0, tiled=True)  19.3 us
    ppermute x12, starting transfers between devices, send(): return lax.ppermute(value, ('ka', 'band'), pairs)  15.1 us
    pallas_call x1, Pallas kernels, exchange(): pl.pallas_call(exchange_kernel, grid=(HALF // TILE,), in_specs=[smem, sme...  11.2 us
    pallas_call x1, Pallas kernels, columns(): pl.pallas_call(columns_kernel, grid=(POINTS // rows,), in_specs=[pl.Block...  8.96 us
    ppermute x12, waiting for transfers between devices, send(): return lax.ppermute(value, ('ka', 'band'), pairs)  6.53 us
    unnamed x8, local copies, waits for them, and re-layouts  2.19 us
    pallas_call x1, Pallas kernels, pick(): pl.pallas_call(pick_kernel, out_shape=jax.ShapeDtypeStruct((ROWS, POINTS)...  1.95 us
    pallas_call x1, Pallas kernels, total(): pl.pallas_call(total_kernel, out_shape=jax.ShapeDtypeStruct((KPTS, 8, 2,...  1.85 us
  transfers between devices with their start and end apart: 12, of which 2 were waited for; matrix products, arithmetic and copies ran while one was open for 0% of the time, Pallas kernels for 13%

profile of v1, /device:TPU:0, one launch (start us, length us, event | category | flops | bytes accessed | tf_op | source)
XLA Modules:
  0.0 67.1 jit_solution(4148499443519526111)
XLA Ops:
  0.0 0.0 copy-start.3
  0.0 0.0 copy-start.2
  0.0 0.0 copy-start.1
  0.0 2.0 %pick_points.1 = f32[16,2048]{1,0:T(8,128)} custom-call(s32[1,2048]{1,0:T(1,128)} %bitcast.5, f32[8,2,4096]{2,1,0:T(2,128)} %bitcast.4), custom_call_target="tpu_custom_call" | custom-call | tf_op jit(solution)/shard_map/pick_points/pallas_call | solution.py:84
  2.0 1.7 %collective-permute-start.9 = (f32[16,2048]{1,0:T(8,128)}, f32[16,2048]{1,0:T(8,128)S(1)}, u32[]{:S(2)}, u32[]{:S(2)}) collective-permute-start(f32[16,2048]{1,0:T(8,128)} %pick_points.1), channel_id=1, source_target_pairs={{0,1},{1,16},{2,3},{3,18},{4,5},{5,20},{6,7},{7,22},{8,25},{9,24},... | collective-permute-start | bytes 393224 | tf_op jit(solution)/shard_map/ppermute | solution.py:60
  3.6 3.4 %collective-permute-start.8 = (f32[16,2048]{1,0:T(8,128)}, f32[16,2048]{1,0:T(8,128)S(1)}, u32[]{:S(2)}, u32[]{:S(2)}) collective-permute-start(f32[16,2048]{1,0:T(8,128)} %pick_points.1), channel_id=1, source_target_pairs={{0,16},{1,1},{2,18},{3,3},{4,20},{5,5},{6,22},{7,7},{8,24},{9,25},... | collective-permute-start | bytes 393224 | tf_op jit(solution)/shard_map/ppermute | solution.py:60
  7.0 6.3 %collective-permute-start.3 = (f32[16,2048]{1,0:T(8,128)}, f32[16,2048]{1,0:T(8,128)S(1)}, u32[]{:S(2)}, u32[]{:S(2)}) collective-permute-start(f32[16,2048]{1,0:T(8,128)} %pick_points.1), channel_id=1, source_target_pairs={{0,6},{1,12},{2,4},{3,14},{4,2},{5,8},{6,0},{7,10},{8,7},{9,15},{1... | collective-permute-start | bytes 393224 | tf_op jit(solution)/shard_map/ppermute | solution.py:60
  13.3 0.0 collective-permute-start.2
  13.3 0.6 collective-permute-start.1
  13.9 0.0 collective-permute-done.9.refs_9_
  13.9 1.6 %collective-permute-start = (f32[16,2048]{1,0:T(8,128)}, f32[16,2048]{1,0:T(8,128)S(1)}, u32[]{:S(2)}, u32[]{:S(2)}) collective-permute-start(f32[16,2048]{1,0:T(8,128)} %pick_points.1), channel_id=1, source_target_pairs={{0,0},{1,10},{2,2},{3,8},{4,4},{5,14},{6,6},{7,12},{8,1},{9,9},{10... | collective-permute-start | bytes 393224 | tf_op jit(solution)/shard_map/ppermute | solution.py:60
  15.5 0.0 collective-permute-done.8.refs_8_
  15.5 0.3 collective-permute-start.11
  15.8 3.1 %collective-permute-done.3.refs_3_ = f32[16,2048]{1,0:T(8,128)S(1)} collective-permute-done((f32[16,2048]{1,0:T(8,128)}, f32[16,2048]{1,0:T(8,128)S(1)}, u32[]{:S(2)}, u32[]{:S(2)}) %collective-permute-start.3) | collective-permute-done | bytes 131104 | tf_op jit(solution)/shard_map/ppermute | solution.py:60
  18.9 0.3 collective-permute-start.10
  19.2 3.4 %collective-permute-done.2.refs_2_ = f32[16,2048]{1,0:T(8,128)S(1)} collective-permute-done((f32[16,2048]{1,0:T(8,128)}, f32[16,2048]{1,0:T(8,128)S(1)}, u32[]{:S(2)}, u32[]{:S(2)}) %collective-permute-start.2) | collective-permute-done | bytes 131104 | tf_op jit(solution)/shard_map/ppermute | solution.py:60
  22.6 0.0 collective-permute-start.7
  22.6 0.0 collective-permute-done.1.refs_1_
  22.6 0.5 collective-permute-start.6
  23.1 0.0 collective-permute-done.refs_0_
  23.1 0.1 collective-permute-start.5
  23.2 0.0 collective-permute-done.11.refs_11_
  23.2 0.4 collective-permute-start.4
  23.6 9.0 %kernel_columns.1.k_ref = bf16[2048,1024]{1,0:T(8,128)(2,1)} custom-call(bf16[2048,2048]{1,0:T(8,128)(2,1)} %k_ref.1), custom_call_target="tpu_custom_call" | custom-call | flops 16777216 | bytes 12582912 | tf_op jit(solution)/shard_map/kernel_columns/pallas_call | solution.py:109
  32.6 0.0 collective-permute-done.10.refs_10_
  32.6 0.0 collective-permute-done.7.refs_7_
  32.6 0.0 collective-permute-done.6.refs_6_
  32.6 0.0 collective-permute-done.5.refs_5_
  32.6 0.0 collective-permute-done.4.refs_4_
  32.6 0.0 copy-done.3
  32.6 0.0 copy-done.2
  32.6 0.0 copy-done.1
  32.6 0.0 copy-start
  32.7 2.2 %copy-done = bf16[2048,1024]{1,0:T(8,128)(2,1)S(1)} copy-done((bf16[2048,1024]{1,0:T(8,128)(2,1)S(1)}, bf16[2048,1024]{1,0:T(8,128)(2,1)}, u32[]{:S(2)}) %copy-start) | copy-done | bytes 4194328
  34.8 11.2 %exchange_terms.1 = f32[16,8,8,128]{3,2,1,0:T(8,128)S(1)} custom-call(s32[16,16]{1,0:T(8,128)S(1)} %copy-done.2, s32[16]{0:T(128)S(1)} %copy-done.3, f32[16,2048]{1,0:T(8,128)S(1)} %copy-done.1, bf16[2048,1024]{1,0:T(8,128)(2,1)S(1)} %copy-done, f32[16,2048]{1,0:T(8,128)S(1)} %collective-permute-done.refs_0_, f32[16,2048]{1,0:T(8,128)S(1)} %collective-permute-done.1.refs_1_, ...), custom_call_target="tpu_custom_call" | custom-call | flops 14000000000 | bytes 8388608 | tf_op jit(solution)/shard_map/exchange_terms/pallas_call | solution.py:210
  46.0 19.3 %all_to_all.5.in_ref = f32[128,8,128]{2,1,0:T(8,128)} all-to-all(f32[128,8,128]{2,1,0:T(8,128)S(1)} %bitcast.3), channel_id=1, replica_groups=mesh['ka'=16,'band'=8] {'ka','band'}, dimensions={0} | all-to-all | bytes 1048576 | tf_op jit(solution)/shard_map/all_to_all | solution.py:259
  65.3 1.8 %total.1 = f32[16,8,2,128]{3,2,1,0:T(2,128)} custom-call(f32[128,8,128]{2,1,0:T(8,128)} %all_to_all.5.in_ref), custom_call_target="tpu_custom_call" | custom-call | tf_op jit(solution)/shard_map/total/pallas_call | solution.py:244
Async XLA Ops:
  0.0 32.6 %copy-start.3 = (s32[16]{0:T(128)S(1)}, s32[16]{0:T(128)}, u32[]{:S(2)}) copy-start(s32[16]{0:T(128)} %occ_ref.1) | copy-start | bytes 196
  0.0 32.6 %copy-start.2 = (s32[16,16]{1,0:T(8,128)S(1)}, s32[16,16]{1,0:T(8,128)}, u32[]{:S(2)}) copy-start(s32[16,16]{1,0:T(8,128)} %table_ref.1) | copy-start | bytes 3076
  0.0 32.6 %copy-start.1 = (f32[16,2048]{1,0:T(8,128)S(1)}, f32[16,2048]{1,0:T(8,128)}, u32[]{:S(2)}) copy-start(f32[16,2048]{1,0:T(8,128)} %weight_ref.1) | copy-start | bytes 393220
  2.0 12.0 %collective-permute-start.9 = (f32[16,2048]{1,0:T(8,128)}, f32[16,2048]{1,0:T(8,128)S(1)}, u32[]{:S(2)}, u32[]{:S(2)}) collective-permute-start(f32[16,2048]{1,0:T(8,128)} %pick_points.1), channel_id=1, source_target_pairs={{0,1},{1,16},{2,3},{3,18},{4,5},{5,20},{6,7},{7,22},{8,25},{9,24},... | collective-permute-start | bytes 393224 | tf_op jit(solution)/shard_map/ppermute | solution.py:60
  3.6 11.9 %collective-permute-start.8 = (f32[16,2048]{1,0:T(8,128)}, f32[16,2048]{1,0:T(8,128)S(1)}, u32[]{:S(2)}, u32[]{:S(2)}) collective-permute-start(f32[16,2048]{1,0:T(8,128)} %pick_points.1), channel_id=1, source_target_pairs={{0,16},{1,1},{2,18},{3,3},{4,20},{5,5},{6,22},{7,7},{8,24},{9,25},... | collective-permute-start | bytes 393224 | tf_op jit(solution)/shard_map/ppermute | solution.py:60
  7.0 11.9 %collective-permute-start.3 = (f32[16,2048]{1,0:T(8,128)}, f32[16,2048]{1,0:T(8,128)S(1)}, u32[]{:S(2)}, u32[]{:S(2)}) collective-permute-start(f32[16,2048]{1,0:T(8,128)} %pick_points.1), channel_id=1, source_target_pairs={{0,6},{1,12},{2,4},{3,14},{4,2},{5,8},{6,0},{7,10},{8,7},{9,15},{1... | collective-permute-start | bytes 393224 | tf_op jit(solution)/shard_map/ppermute | solution.py:60
  13.3 9.3 %collective-permute-start.2 = (f32[16,2048]{1,0:T(8,128)}, f32[16,2048]{1,0:T(8,128)S(1)}, u32[]{:S(2)}, u32[]{:S(2)}) collective-permute-start(f32[16,2048]{1,0:T(8,128)} %pick_points.1), channel_id=1, source_target_pairs={{0,4},{1,14},{2,6},{3,12},{4,0},{5,10},{6,2},{7,8},{8,5},{9,13},{1... | collective-permute-start | bytes 393224 | tf_op jit(solution)/shard_map/ppermute | solution.py:60
  13.3 9.3 %collective-permute-start.1 = (f32[16,2048]{1,0:T(8,128)}, f32[16,2048]{1,0:T(8,128)S(1)}, u32[]{:S(2)}, u32[]{:S(2)}) collective-permute-start(f32[16,2048]{1,0:T(8,128)} %pick_points.1), channel_id=1, source_target_pairs={{0,2},{1,8},{2,0},{3,10},{4,6},{5,12},{6,4},{7,14},{8,3},{9,11},{1... | collective-permute-start | bytes 393224 | tf_op jit(solution)/shard_map/ppermute | solution.py:60
  13.9 9.2 %collective-permute-start = (f32[16,2048]{1,0:T(8,128)}, f32[16,2048]{1,0:T(8,128)S(1)}, u32[]{:S(2)}, u32[]{:S(2)}) collective-permute-start(f32[16,2048]{1,0:T(8,128)} %pick_points.1), channel_id=1, source_target_pairs={{0,0},{1,10},{2,2},{3,8},{4,4},{5,14},{6,6},{7,12},{8,1},{9,9},{10... | collective-permute-start | bytes 393224 | tf_op jit(solution)/shard_map/ppermute | solution.py:60
  15.5 7.7 %collective-permute-start.11 = (f32[16,2048]{1,0:T(8,128)S(1)}, f32[16,2048]{1,0:T(8,128)S(1)}, u32[]{:S(2)}, u32[]{:S(2)}) collective-permute-start(f32[16,2048]{1,0:T(8,128)S(1)} %collective-permute-done.9.refs_9_), channel_id=1, source_target_pairs={{0,8},{1,9},{2,10},{3,11},{4,12},{5,13},{6,14},{7,15},{8,0},{9,1},... | collective-permute-start | bytes 393224 | tf_op jit(solution)/shard_map/ppermute | solution.py:60
  18.9 13.6 %collective-permute-start.10 = (f32[16,2048]{1,0:T(8,128)S(1)}, f32[16,2048]{1,0:T(8,128)S(1)}, u32[]{:S(2)}, u32[]{:S(2)}) collective-permute-start(f32[16,2048]{1,0:T(8,128)S(1)} %collective-permute-done.8.refs_8_), channel_id=1, source_target_pairs={{0,8},{1,9},{2,10},{3,11},{4,12},{5,13},{6,14},{7,15},{8,0},{9,1},... | collective-permute-start | bytes 393224 | tf_op jit(solution)/shard_map/ppermute | solution.py:60
  22.6 10.0 %collective-permute-start.7 = (f32[16,2048]{1,0:T(8,128)S(1)}, f32[16,2048]{1,0:T(8,128)S(1)}, u32[]{:S(2)}, u32[]{:S(2)}) collective-permute-start(f32[16,2048]{1,0:T(8,128)S(1)} %collective-permute-done.3.refs_3_), channel_id=1, source_target_pairs={{0,8},{1,9},{2,10},{3,11},{4,12},{5,13},{6,14},{7,15},{8,0},{9,1},... | collective-permute-start | bytes 393224 | tf_op jit(solution)/shard_map/ppermute | solution.py:60
  22.6 10.0 %collective-permute-start.6 = (f32[16,2048]{1,0:T(8,128)S(1)}, f32[16,2048]{1,0:T(8,128)S(1)}, u32[]{:S(2)}, u32[]{:S(2)}) collective-permute-start(f32[16,2048]{1,0:T(8,128)S(1)} %collective-permute-done.2.refs_2_), channel_id=1, source_target_pairs={{0,8},{1,9},{2,10},{3,11},{4,12},{5,13},{6,14},{7,15},{8,0},{9,1},... | collective-permute-start | bytes 393224 | tf_op jit(solution)/shard_map/ppermute | solution.py:60
  23.1 9.5 %collective-permute-start.5 = (f32[16,2048]{1,0:T(8,128)S(1)}, f32[16,2048]{1,0:T(8,128)S(1)}, u32[]{:S(2)}, u32[]{:S(2)}) collective-permute-start(f32[16,2048]{1,0:T(8,128)S(1)} %collective-permute-done.1.refs_1_), channel_id=1, source_target_pairs={{0,8},{1,9},{2,10},{3,11},{4,12},{5,13},{6,14},{7,15},{8,0},{9,1},... | collective-permute-start | bytes 393224 | tf_op jit(solution)/shard_map/ppermute | solution.py:60
  23.2 9.4 %collective-permute-start.4 = (f32[16,2048]{1,0:T(8,128)S(1)}, f32[16,2048]{1,0:T(8,128)S(1)}, u32[]{:S(2)}, u32[]{:S(2)}) collective-permute-start(f32[16,2048]{1,0:T(8,128)S(1)} %collective-permute-done.refs_0_), channel_id=1, source_target_pairs={{0,8},{1,9},{2,10},{3,11},{4,12},{5,13},{6,14},{7,15},{8,0},{9,1},... | collective-permute-start | bytes 393224 | tf_op jit(solution)/shard_map/ppermute | solution.py:60
  32.6 2.2 %copy-start = (bf16[2048,1024]{1,0:T(8,128)(2,1)S(1)}, bf16[2048,1024]{1,0:T(8,128)(2,1)}, u32[]{:S(2)}) copy-start(bf16[2048,1024]{1,0:T(8,128)(2,1)} %kernel_columns.1.k_ref) | copy-start | bytes 12582916

commit v2 on v1

v2 whole, which is shorter than its diff:
```python
import jax
import jax.numpy as jnp
from jax import lax
from jax.experimental import pallas as pl
from jax.experimental.pallas import tpu as pltpu
from jax.sharding import Mesh
from jax.sharding import PartitionSpec as P

STEPS = 3
KPTS = 16
BLOCKS = 8
ROWS = 16
POINTS = 2048
TILES = 4
WIDE = 2
DEPTH = 128
CHUNK = 256
FACTOR = -1.0 / (STEPS * 64) ** 0.5
F32, BF16 = jnp.float32, jnp.bfloat16


def device(i, c, zh, y):
    return ((i % 8) * 2 + c) * BLOCKS + zh * 4 + y % 4


def everyone():
    return [(i, c, zh, y) for i in range(8) for c in range(2) for zh in range(2) for y in range(4)]


def gather_pairs(tz, ty):
    pairs = []
    for i, c, zh, y in everyone():
        if y % 2 == c:
            to = device(i, c, zh ^ tz, y + 2 * ty)
        else:
            to = device(i, 1 - c, zh ^ tz, (y ^ 1) + 2 * ty)
        pairs.append((device(i, c, zh, y), to))
    return pairs


def own_band_pairs():
    pairs = []
    for i, c, zh, y in everyone():
        stay = c == 0 and y % 2 == 1
        pairs.append((device(i, c, zh, y), device(i if stay else i + 1, c, zh, y)))
    return pairs


def next_band_pairs():
    pairs = []
    for i, c, zh, y in everyone():
        stay = c == 0 and y % 2 == 0
        pairs.append((device(i, c, zh, y), device(i if stay else i + 1, c, zh, y ^ 1)))
    return pairs


def core_pairs():
    return [(device(i, c, zh, y), device(i, 1 - c, zh, y)) for i, c, zh, y in everyone()]


def send(value, pairs):
    return lax.ppermute(value, ("i", "core", "band"), pairs)


def place():
    band = lax.axis_index("band")
    return lax.axis_index("i"), lax.axis_index("core"), band // 4, band % 4, band


def pick_kernel(index_ref, orb_ref, out_ref):
    for j in range(POINTS // 128):
        idx = jnp.broadcast_to(index_ref[:, j * 128 : (j + 1) * 128], (8, 128)) & 127
        low = lax.broadcasted_iota(jnp.int32, (8, 128), 1) < 64
        for part in range(2):
            left = orb_ref[:, part, 2 * j * 128 : (2 * j + 1) * 128]
            right = orb_ref[:, part, (2 * j + 1) * 128 : (2 * j + 2) * 128]
            got = jnp.where(
                low,
                jnp.take_along_axis(left, idx, axis=1, mode="promise_in_bounds"),
                jnp.take_along_axis(right, idx, axis=1, mode="promise_in_bounds"),
            )
            out_ref[part * 8 : part * 8 + 8, j * 128 : (j + 1) * 128] = got


def pick(orbitals, point_index):
    return pl.pallas_call(
        pick_kernel,
        out_shape=jax.ShapeDtypeStruct((ROWS, POINTS), F32),
        name="pick_points",
    )(point_index.reshape(1, POINTS), orbitals)


def split(value):
    high = value.astype(BF16)
    return high, (value - high.astype(F32)).astype(BF16)


def product_kernel(core_ref, table_ref, occ_ref, weight_ref, *refs):
    k_refs, refs = refs[:WIDE], refs[WIDE:]
    mine, theirs, before = refs[0], refs[1], refs[2:6]
    high_ref, low_ref, p_ref, pt_ref, f_ref = refs[6:]
    i, c, zh, y, band = place()
    parity = y % 2
    kpoint = 2 * i + parity
    same = c == parity
    own_step = jnp.where(same, 2, 1)
    points = [lax.rem(kpoint - s + KPTS, KPTS) for s in (0, own_step, 3 - own_step)]

    @pl.when(pl.program_id(0) == 0)
    def _():
        f_ref[...] = jnp.zeros_like(f_ref)
        for g in range(STEPS):
            f_ref[pl.ds(g, 1), :] = weight_ref[pl.ds(table_ref[kpoint, points[g]], 1), :]
        p_ref[96:, :] = jnp.zeros((DEPTH - 96, POINTS), F32)
        p_ref[0:16, :] = jnp.where(same, mine[...], theirs[...])
        p_ref[16:32, :] = jnp.where(same, theirs[...], mine[...])
        for n in range(4):
            p_ref[32 + 16 * n : 48 + 16 * n, :] = before[n][...]
        for j in range(POINTS // 128):
            cols = slice(j * 128, (j + 1) * 128)
            scaled = jnp.concatenate(
                [p_ref[32 * g : 32 * g + 32, cols] * f_ref[g : g + 1, cols] for g in range(STEPS)] + [p_ref[96:, cols]], axis=0
            )
            high, low = split(scaled.T)
            pt_ref[cols, 0:128] = high
            pt_ref[cols, 128:256] = high
            pt_ref[cols, 256:384] = low

    row = lax.broadcasted_iota(jnp.int32, (32, 128), 0)
    number = jnp.where(row < 16, band, band ^ 1) * 8 + (row & 7)
    fill = [jnp.zeros((DEPTH - 96, 128), F32)]
    sides = []
    for j in range(WIDE):
        here = pl.ds(pl.multiple_of((2 * (pl.program_id(0) * WIDE + j) + c) * 128, 128), 128)
        f_here = f_ref[:, here]
        plain, turned = [], []
        for g in range(STEPS):
            live = number < occ_ref[points[g]]
            value = jnp.where(live, p_ref[32 * g : 32 * g + 32, here] * f_here[g : g + 1], 0.0)
            plain.append(value)
            turned += [value[8:16], -value[0:8], value[24:32], -value[16:24]]
        sides += [jnp.concatenate(plain + fill, axis=0), jnp.concatenate(turned + fill, axis=0)]
    high, low = split(jnp.concatenate(sides, axis=1))
    w = jnp.concatenate([high, low, high], axis=0)
    for n in range(POINTS // CHUNK):
        rows = slice(n * CHUNK, (n + 1) * CHUNK)
        e = jnp.dot(pt_ref[rows, :], w, preferred_element_type=F32)
        for j in range(WIDE):
            kf = k_refs[j][rows, :].astype(F32)
            for part in range(2):
                cols = slice((2 * j + part) * 128, (2 * j + part + 1) * 128)
                high, low = split(e[:, cols] * kf)
                high_ref[pl.program_id(0), rows, cols] = high
                low_ref[pl.program_id(0), rows, cols] = low


WHOLE = pl.BlockSpec(memory_space=pltpu.VMEM)
SMEM = pl.BlockSpec(memory_space=pltpu.SMEM)


def product(core, q_table, occ_count, q_weight, kernel, mine, theirs, before):
    return pl.pallas_call(
        product_kernel,
        grid_spec=pltpu.PrefetchScalarGridSpec(
            num_scalar_prefetch=1,
            grid=(TILES,),
            in_specs=[SMEM, SMEM, WHOLE]
            + [pl.BlockSpec((POINTS, 128), lambda u, core, j=j: (0, 2 * (u * WIDE + j) + core[0])) for j in range(WIDE)]
            + [WHOLE] * 6,
            out_specs=[WHOLE, WHOLE],
            scratch_shapes=[
                pltpu.VMEM((DEPTH, POINTS), F32),
                pltpu.VMEM((POINTS, 3 * DEPTH), BF16),
                pltpu.VMEM((8, POINTS), F32),
            ],
        ),
        out_shape=[jax.ShapeDtypeStruct((TILES, POINTS, WIDE * 256), BF16)] * 2,
        compiler_params=pltpu.CompilerParams(vmem_limit_bytes=28 * 2**20),
        cost_estimate=pl.CostEstimate(flops=7 * 10**9, bytes_accessed=8 * 2**20, transcendentals=0),
        name="kernel_product",
    )(core, q_table, occ_count, q_weight, *[kernel] * WIDE, mine, theirs, *before)


def apply_kernel(high_ref, low_ref, *refs):
    mine, theirs, out_ref, x_ref = refs[0:4], refs[4:8], refs[8], refs[9]
    i, c, zh, y, band = place()
    same = c == y % 2
    for group, first in ((mine, jnp.where(same, band, band ^ 1)), (theirs, jnp.where(same, band ^ 1, band))):
        for t, ref in enumerate(group):
            block = first ^ (4 * (t // 2) + 2 * (t % 2))
            high, low = split(ref[...])
            row = pl.multiple_of(block * ROWS, ROWS)
            x_ref[pl.ds(row, ROWS), :] = high
            x_ref[pl.ds(pl.multiple_of(128 + row, ROWS), ROWS), :] = low
    for u in range(TILES):
        first = jnp.dot(x_ref[...], high_ref[u], preferred_element_type=F32)
        second = jnp.dot(x_ref[0:128, :], low_ref[u], preferred_element_type=F32)
        r = first[0:128] + first[128:256] + second
        for b in range(BLOCKS):
            top, bottom = r[b * ROWS : b * ROWS + 8], r[b * ROWS + 8 : b * ROWS + 16]
            for j in range(WIDE):
                re, im = slice(j * 256, j * 256 + 128), slice(j * 256 + 128, j * 256 + 256)
                out_ref[u * WIDE + j, b, 0] = top[:, re] - bottom[:, im]
                out_ref[u * WIDE + j, b, 1] = top[:, im] + bottom[:, re]


def apply(high, low, mine, theirs):
    return pl.pallas_call(
        apply_kernel,
        in_specs=[WHOLE] * 10,
        out_specs=WHOLE,
        out_shape=jax.ShapeDtypeStruct((TILES * WIDE, BLOCKS, 2, 8, 128), F32),
        scratch_shapes=[pltpu.VMEM((256, POINTS), BF16)],
        compiler_params=pltpu.CompilerParams(vmem_limit_bytes=28 * 2**20),
        cost_estimate=pl.CostEstimate(flops=4 * 10**9, bytes_accessed=18 * 2**20, transcendentals=0),
        name="apply_orbitals",
    )(high, low, *mine, *theirs)


def total_kernel(in_ref, out_ref):
    for k in range(KPTS):
        i, parity = k // 2, k % 2
        for part in range(2):
            parts = [in_ref[i * BLOCKS + zh * 4 + parity + 2 * h, part] for zh in range(2) for h in range(2)]
            out_ref[k, :, part, :] = ((parts[0] + parts[1]) + (parts[2] + parts[3])) * FACTOR


def total(parts):
    return pl.pallas_call(
        total_kernel,
        out_shape=jax.ShapeDtypeStruct((KPTS, 8, 2, 128), F32),
        name="total",
    )(parts)


def body(orbitals, point_index, kernel, q_weight, q_table, occ_count):
    core = lax.axis_index("core").astype(jnp.int32).reshape(1)
    kernel, q_weight, q_table, occ_count = (
        pltpu.with_memory_space_constraint(value, pltpu.HBM) for value in (kernel, q_weight, q_table, occ_count)
    )
    block = pick(orbitals[0], point_index)
    far = [send(block, gather_pairs(1, t)) for t in range(2)]
    near = [send(block, gather_pairs(0, t)) for t in range(2)]
    before = [send(block, own_band_pairs()), send(block, next_band_pairs())]
    before_theirs = [send(value, core_pairs()) for value in before]
    near_theirs = [send(value, core_pairs()) for value in near]
    high, low = product(core, q_table, occ_count, q_weight, kernel, near[0], near_theirs[0], before + before_theirs)
    far[0], far[1], high, low = lax.optimization_barrier((far[0], far[1], high, low))
    far_theirs = [send(value, core_pairs()) for value in far]
    parts = apply(high, low, near + far, near_theirs + far_theirs)
    got = lax.all_to_all(parts.reshape(64, 2, 8, 128), ("i", "band"), 0, 0, tiled=True)
    return total(got)


def solution(mesh):
    split_mesh = Mesh(mesh.devices.reshape(8, 2, BLOCKS), ("i", "core", "band"))
    ka = ("i", "core")
    placed = (P(ka, "band", None, None), P(), P(), P(), P(), P())
    return jax.shard_map(body, mesh=split_mesh, in_specs=placed, out_specs=P(None, "band", None, ka), check_vma=False)
```

time: 67.6 us -> 58.2 us (0.86)
  Pallas kernels: 23.9 us -> 14.8 us
  waiting for transfers between devices: 6.53 us -> 2.58 us
  blocking collectives: 19.3 us -> 22.6 us
  starting transfers between devices: 15.1 us -> 17.9 us
  local copies, waits for them, and re-layouts: 2.19 us -> 0 us
    pallas_call x2, Pallas kernels: 20.1 us -> 11.1 us  [the longest x1 7.58 us: product(): pl.pallas_call(product_kernel, grid_spec=pltpu.PrefetchScalarGridSpec(num...]
    ppermute x12, waiting for transfers between devices: 6.53 us -> 2.58 us  [send(): return lax.ppermute(value, ('i', 'core', 'band'), pairs)]
    all_to_all x1, blocking collectives: 19.3 us -> 22.6 us  [body(): lax.all_to_all(parts.reshape(64, 2, 8, 128), ('i', 'band'), 0, 0, tiled=T...]
    ppermute x12, starting transfers between devices: 15.1 us -> 17.9 us  [send(): return lax.ppermute(value, ('i', 'core', 'band'), pairs)]
    unnamed x8 -> x0, local copies, waits for them, and re-layouts: 2.19 us -> none
  transfers between devices with their start and end apart: 12 -> 12, of which waited for: 2 -> 3; matrix products, arithmetic and copies ran while one was open for 0% -> 0% of each run, Pallas kernels for 13% -> 13%
where the time goes in v2:
time: 58.2 us; the launch traced here: 57.9 us
  blocking collectives  22.6 us (39%)
  starting transfers between devices  17.9 us (31%)
  Pallas kernels  14.8 us (25%)
  waiting for transfers between devices  2.58 us (4%)
    all_to_all x1, blocking collectives, body(): lax.all_to_all(parts.reshape(64, 2, 8, 128), ('i', 'band'), 0, 0, tiled=T...  22.6 us
    ppermute x12, starting transfers between devices, send(): return lax.ppermute(value, ('i', 'core', 'band'), pairs)  17.9 us
    pallas_call x1, Pallas kernels, product(): pl.pallas_call(product_kernel, grid_spec=pltpu.PrefetchScalarGridSpec(num...  7.58 us
    pallas_call x1, Pallas kernels, apply(): pl.pallas_call(apply_kernel, in_specs=[WHOLE] * 10, out_specs=WHOLE, out_...  3.54 us
    ppermute x12, waiting for transfers between devices, send(): return lax.ppermute(value, ('i', 'core', 'band'), pairs)  2.58 us
    pallas_call x1, Pallas kernels, pick(): pl.pallas_call(pick_kernel, out_shape=jax.ShapeDtypeStruct((ROWS, POINTS)...  1.92 us
    pallas_call x1, Pallas kernels, total(): pl.pallas_call(total_kernel, out_shape=jax.ShapeDtypeStruct((KPTS, 8, 2,...  1.79 us
  transfers between devices with their start and end apart: 12, of which 3 were waited for; matrix products, arithmetic and copies ran while one was open for 0% of the time, Pallas kernels for 13%

profile of v2, /device:TPU:0, one launch (start us, length us, event | category | flops | bytes accessed | tf_op | source)
XLA Modules:
  0.0 57.9 jit_solution(9755600160125843075)
XLA Ops:
  0.0 1.9 %pick_points.1 = f32[16,2048]{1,0:T(8,128)} custom-call(s32[1,2048]{1,0:T(1,128)} %bitcast.6, f32[8,2,4096]{2,1,0:T(2,128)} %bitcast.5), custom_call_target="tpu_custom_call" | custom-call | tf_op jit(solution)/shard_map/pick_points/pallas_call | solution.py:86
  1.9 1.7 %collective-permute-start.5 = (f32[16,2048]{1,0:T(8,128)}, f32[16,2048]{1,0:T(8,128)S(1)}, u32[]{:S(2)}, u32[]{:S(2)}) collective-permute-start(f32[16,2048]{1,0:T(8,128)} %pick_points.1), channel_id=1, source_target_pairs={{0,1},{1,16},{2,3},{3,18},{4,5},{5,20},{6,7},{7,22},{8,25},{9,24},... | collective-permute-start | bytes 393224 | tf_op jit(solution)/shard_map/ppermute | solution.py:62
  3.6 3.4 %collective-permute-start.4 = (f32[16,2048]{1,0:T(8,128)}, f32[16,2048]{1,0:T(8,128)S(1)}, u32[]{:S(2)}, u32[]{:S(2)}) collective-permute-start(f32[16,2048]{1,0:T(8,128)} %pick_points.1), channel_id=1, source_target_pairs={{0,16},{1,1},{2,18},{3,3},{4,20},{5,5},{6,22},{7,7},{8,24},{9,25},... | collective-permute-start | bytes 393224 | tf_op jit(solution)/shard_map/ppermute | solution.py:62
  7.0 1.6 %collective-permute-start.2 = (f32[16,2048]{1,0:T(8,128)}, f32[16,2048]{1,0:T(8,128)S(1)}, u32[]{:S(2)}, u32[]{:S(2)}) collective-permute-start(f32[16,2048]{1,0:T(8,128)} %pick_points.1), channel_id=1, source_target_pairs={{0,0},{1,8},{2,2},{3,10},{4,4},{5,12},{6,6},{7,14},{8,1},{9,9},{10... | collective-permute-start | bytes 393224 | tf_op jit(solution)/shard_map/ppermute | solution.py:62
  8.5 2.9 %collective-permute-start.8 = (f32[16,2048]{1,0:T(8,128)}, f32[16,2048]{1,0:T(8,128)S(1)}, u32[]{:S(2)}, u32[]{:S(2)}) collective-permute-start(f32[16,2048]{1,0:T(8,128)} %pick_points.1), channel_id=1, source_target_pairs={{0,2},{1,10},{2,0},{3,8},{4,6},{5,14},{6,4},{7,12},{8,3},{9,11},{1... | collective-permute-start | bytes 393224 | tf_op jit(solution)/shard_map/ppermute | solution.py:62
  11.4 0.0 collective-permute-done.5.refs_5_
  11.4 0.9 %collective-permute-start.7 = (f32[16,2048]{1,0:T(8,128)S(1)}, f32[16,2048]{1,0:T(8,128)S(1)}, u32[]{:S(2)}, u32[]{:S(2)}) collective-permute-start(f32[16,2048]{1,0:T(8,128)S(1)} %collective-permute-done.5.refs_5_), channel_id=1, source_target_pairs={{0,8},{1,9},{2,10},{3,11},{4,12},{5,13},{6,14},{7,15},{8,0},{9,1},... | collective-permute-start | bytes 393224 | tf_op jit(solution)/shard_map/ppermute | solution.py:62
  12.4 1.3 %collective-permute-done.4.refs_4_ = f32[16,2048]{1,0:T(8,128)S(1)} collective-permute-done((f32[16,2048]{1,0:T(8,128)}, f32[16,2048]{1,0:T(8,128)S(1)}, u32[]{:S(2)}, u32[]{:S(2)}) %collective-permute-start.4) | collective-permute-done | bytes 131104 | tf_op jit(solution)/shard_map/ppermute | solution.py:62
  13.7 0.0 collective-permute-start.6
  13.7 0.0 collective-permute-done.2.refs_2_.refs_0_
  13.7 1.6 %collective-permute-start.3 = (f32[16,2048]{1,0:T(8,128)S(1)}, f32[16,2048]{1,0:T(8,128)S(1)}, u32[]{:S(2)}, u32[]{:S(2)}) collective-permute-start(f32[16,2048]{1,0:T(8,128)S(1)} %collective-permute-done.2.refs_2_.refs_0_), channel_id=1, source_target_pairs={{0,8},{1,9},{2,10},{3,11},{4,12},{5,13},{6,14},{7,15},{8,0},{9,1},... | collective-permute-start | bytes 393224 | tf_op jit(solution)/shard_map/ppermute | solution.py:62
  15.3 5.1 %collective-permute-start.1 = (f32[16,2048]{1,0:T(8,128)}, f32[16,2048]{1,0:T(8,128)S(1)}, u32[]{:S(2)}, u32[]{:S(2)}) collective-permute-start(f32[16,2048]{1,0:T(8,128)} %pick_points.1), channel_id=1, source_target_pairs={{0,6},{1,14},{2,4},{3,12},{4,2},{5,10},{6,0},{7,8},{8,7},{9,15},{1... | collective-permute-start | bytes 393224 | tf_op jit(solution)/shard_map/ppermute | solution.py:62
  20.4 0.0 collective-permute-done.8.refs_1_
  20.4 0.0 collective-permute-start
  20.4 0.0 collective-permute-done.7.refs_7_
  20.4 0.1 collective-permute-start.9
  20.5 0.0 collective-permute-done.6.refs_6_
  20.5 0.0 collective-permute-done.3.refs_3_.refs_4_
  20.5 7.6 %kernel_product.1 = (bf16[4,2048,512]{2,1,0:T(8,128)(2,1)S(1)}, bf16[4,2048,512]{2,1,0:T(8,128)(2,1)S(1)}) custom-call(s32[1]{0:T(128)} %bitcast.2.core_ref, s32[16,16]{1,0:T(8,128)} %table_ref.1, s32[16]{0:T(128)} %occ_ref.1, f32[16,2048]{1,0:T(8,128)} %weight_ref.1, bf16[2048,2048]{1,0:T(8,128)(2,1)} %refs_1_.1, bf16[2048,2048]{1,0:T(8,128)(2,1)} %refs_1_.1, ...), custom_call_target="tpu_custom_call" | custom-call | flops 7000000000 | bytes 8388608 | tf_op jit(solution)/shard_map/kernel_product/pallas_call | solution.py:162
  28.1 0.0 collective-permute-done.1.refs_3_
  28.1 0.0 collective-permute-done.refs_2_
  28.1 0.5 collective-permute-start.10
  28.7 0.1 collective-permute-start.11
  28.8 0.0 collective-permute-done.9.refs_5_
  28.8 0.9 %collective-permute-done.10.refs_6_ = f32[16,2048]{1,0:T(8,128)S(1)} collective-permute-done((f32[16,2048]{1,0:T(8,128)S(1)}, f32[16,2048]{1,0:T(8,128)S(1)}, u32[]{:S(2)}, u32[]{:S(2)}) %collective-permute-start.10) | collective-permute-done | bytes 131104 | tf_op jit(solution)/shard_map/ppermute | solution.py:62
  29.7 0.4 collective-permute-done.11.refs_7_
  30.0 3.5 %apply_orbitals.1 = f32[8,8,2,8,128]{4,3,2,1,0:T(8,128)S(1)} custom-call(bf16[4,2048,512]{2,1,0:T(8,128)(2,1)S(1)} %get-tuple-element.13.high_ref, bf16[4,2048,512]{2,1,0:T(8,128)(2,1)S(1)} %get-tuple-element.14.low_ref, f32[16,2048]{1,0:T(8,128)S(1)} %collective-permute-done.2.refs_2_.refs_0_, f32[16,2048]{1,0:T(8,128)S(1)} %collective-permute-done.8.refs_1_, ...), custom_call_target="tpu_custom_call" | custom-call | flops 4000000000 | bytes 18874368 | tf_op jit(solution)/shard_map/apply_orbitals/pallas_call | solution.py:208
  33.6 22.6 %all_to_all.5.in_ref = f32[64,2,8,128]{3,2,1,0:T(8,128)} all-to-all(f32[64,2,8,128]{3,2,1,0:T(8,128)S(1)} %bitcast.4), channel_id=1, replica_groups=mesh['i'=8,'core'=2,'band'=8] {'i','band'}, dimensions={0} | all-to-all | bytes 1048576 | tf_op jit(solution)/shard_map/all_to_all | solution.py:251
  56.1 1.8 %total.1 = f32[16,8,2,128]{3,2,1,0:T(2,128)} custom-call(f32[64,2,8,128]{3,2,1,0:T(8,128)} %all_to_all.5.in_ref), custom_call_target="tpu_custom_call" | custom-call | tf_op jit(solution)/shard_map/total/pallas_call | solution.py:229
Async XLA Ops:
  1.9 9.5 %collective-permute-start.5 = (f32[16,2048]{1,0:T(8,128)}, f32[16,2048]{1,0:T(8,128)S(1)}, u32[]{:S(2)}, u32[]{:S(2)}) collective-permute-start(f32[16,2048]{1,0:T(8,128)} %pick_points.1), channel_id=1, source_target_pairs={{0,1},{1,16},{2,3},{3,18},{4,5},{5,20},{6,7},{7,22},{8,25},{9,24},... | collective-permute-start | bytes 393224 | tf_op jit(solution)/shard_map/ppermute | solution.py:62
  3.6 10.1 %collective-permute-start.4 = (f32[16,2048]{1,0:T(8,128)}, f32[16,2048]{1,0:T(8,128)S(1)}, u32[]{:S(2)}, u32[]{:S(2)}) collective-permute-start(f32[16,2048]{1,0:T(8,128)} %pick_points.1), channel_id=1, source_target_pairs={{0,16},{1,1},{2,18},{3,3},{4,20},{5,5},{6,22},{7,7},{8,24},{9,25},... | collective-permute-start | bytes 393224 | tf_op jit(solution)/shard_map/ppermute | solution.py:62
  7.0 6.7 %collective-permute-start.2 = (f32[16,2048]{1,0:T(8,128)}, f32[16,2048]{1,0:T(8,128)S(1)}, u32[]{:S(2)}, u32[]{:S(2)}) collective-permute-start(f32[16,2048]{1,0:T(8,128)} %pick_points.1), channel_id=1, source_target_pairs={{0,0},{1,8},{2,2},{3,10},{4,4},{5,12},{6,6},{7,14},{8,1},{9,9},{10... | collective-permute-start | bytes 393224 | tf_op jit(solution)/shard_map/ppermute | solution.py:62
  8.5 11.9 %collective-permute-start.8 = (f32[16,2048]{1,0:T(8,128)}, f32[16,2048]{1,0:T(8,128)S(1)}, u32[]{:S(2)}, u32[]{:S(2)}) collective-permute-start(f32[16,2048]{1,0:T(8,128)} %pick_points.1), channel_id=1, source_target_pairs={{0,2},{1,10},{2,0},{3,8},{4,6},{5,14},{6,4},{7,12},{8,3},{9,11},{1... | collective-permute-start | bytes 393224 | tf_op jit(solution)/shard_map/ppermute | solution.py:62
  11.4 9.0 %collective-permute-start.7 = (f32[16,2048]{1,0:T(8,128)S(1)}, f32[16,2048]{1,0:T(8,128)S(1)}, u32[]{:S(2)}, u32[]{:S(2)}) collective-permute-start(f32[16,2048]{1,0:T(8,128)S(1)} %collective-permute-done.5.refs_5_), channel_id=1, source_target_pairs={{0,8},{1,9},{2,10},{3,11},{4,12},{5,13},{6,14},{7,15},{8,0},{9,1},... | collective-permute-start | bytes 393224 | tf_op jit(solution)/shard_map/ppermute | solution.py:62
  13.7 6.8 %collective-permute-start.6 = (f32[16,2048]{1,0:T(8,128)S(1)}, f32[16,2048]{1,0:T(8,128)S(1)}, u32[]{:S(2)}, u32[]{:S(2)}) collective-permute-start(f32[16,2048]{1,0:T(8,128)S(1)} %collective-permute-done.4.refs_4_), channel_id=1, source_target_pairs={{0,8},{1,9},{2,10},{3,11},{4,12},{5,13},{6,14},{7,15},{8,0},{9,1},... | collective-permute-start | bytes 393224 | tf_op jit(solution)/shard_map/ppermute | solution.py:62
  13.7 6.8 %collective-permute-start.3 = (f32[16,2048]{1,0:T(8,128)S(1)}, f32[16,2048]{1,0:T(8,128)S(1)}, u32[]{:S(2)}, u32[]{:S(2)}) collective-permute-start(f32[16,2048]{1,0:T(8,128)S(1)} %collective-permute-done.2.refs_2_.refs_0_), channel_id=1, source_target_pairs={{0,8},{1,9},{2,10},{3,11},{4,12},{5,13},{6,14},{7,15},{8,0},{9,1},... | collective-permute-start | bytes 393224 | tf_op jit(solution)/shard_map/ppermute | solution.py:62
  15.3 12.8 %collective-permute-start.1 = (f32[16,2048]{1,0:T(8,128)}, f32[16,2048]{1,0:T(8,128)S(1)}, u32[]{:S(2)}, u32[]{:S(2)}) collective-permute-start(f32[16,2048]{1,0:T(8,128)} %pick_points.1), channel_id=1, source_target_pairs={{0,6},{1,14},{2,4},{3,12},{4,2},{5,10},{6,0},{7,8},{8,7},{9,15},{1... | collective-permute-start | bytes 393224 | tf_op jit(solution)/shard_map/ppermute | solution.py:62
  20.4 7.7 %collective-permute-start = (f32[16,2048]{1,0:T(8,128)}, f32[16,2048]{1,0:T(8,128)S(1)}, u32[]{:S(2)}, u32[]{:S(2)}) collective-permute-start(f32[16,2048]{1,0:T(8,128)} %pick_points.1), channel_id=1, source_target_pairs={{0,4},{1,12},{2,6},{3,14},{4,0},{5,8},{6,2},{7,10},{8,5},{9,13},{1... | collective-permute-start | bytes 393224 | tf_op jit(solution)/shard_map/ppermute | solution.py:62
  20.4 8.4 %collective-permute-start.9 = (f32[16,2048]{1,0:T(8,128)S(1)}, f32[16,2048]{1,0:T(8,128)S(1)}, u32[]{:S(2)}, u32[]{:S(2)}) collective-permute-start(f32[16,2048]{1,0:T(8,128)S(1)} %collective-permute-done.8.refs_1_), channel_id=1, source_target_pairs={{0,8},{1,9},{2,10},{3,11},{4,12},{5,13},{6,14},{7,15},{8,0},{9,1},... | collective-permute-start | bytes 393224 | tf_op jit(solution)/shard_map/ppermute | solution.py:62
  28.1 1.5 %collective-permute-start.10 = (f32[16,2048]{1,0:T(8,128)S(1)}, f32[16,2048]{1,0:T(8,128)S(1)}, u32[]{:S(2)}, u32[]{:S(2)}) collective-permute-start(f32[16,2048]{1,0:T(8,128)S(1)} %collective-permute-done.refs_2_), channel_id=1, source_target_pairs={{0,8},{1,9},{2,10},{3,11},{4,12},{5,13},{6,14},{7,15},{8,0},{9,1},... | collective-permute-start | bytes 393224 | tf_op jit(solution)/shard_map/ppermute | solution.py:62
  28.7 1.3 %collective-permute-start.11 = (f32[16,2048]{1,0:T(8,128)S(1)}, f32[16,2048]{1,0:T(8,128)S(1)}, u32[]{:S(2)}, u32[]{:S(2)}) collective-permute-start(f32[16,2048]{1,0:T(8,128)S(1)} %collective-permute-done.1.refs_3_), channel_id=1, source_target_pairs={{0,8},{1,9},{2,10},{3,11},{4,12},{5,13},{6,14},{7,15},{8,0},{9,1},... | collective-permute-start | bytes 393224 | tf_op jit(solution)/shard_map/ppermute | solution.py:62

commit v3 on v2

--- a/solution.py
+++ b/solution.py
@@ -13,8 +13,8 @@
 POINTS = 2048
 TILES = 4
 WIDE = 2
-DEPTH = 128
-CHUNK = 256
+DEPTH = 256
+CHUNK = 512
 FACTOR = -1.0 / (STEPS * 64) ** 0.5
 F32, BF16 = jnp.float32, jnp.bfloat16
 
@@ -85,7 +85,7 @@
 def pick(orbitals, point_index):
     return pl.pallas_call(
         pick_kernel,
-        out_shape=jax.ShapeDtypeStruct((ROWS, POINTS), F32),
+        out_shape=pltpu.VMEM((ROWS, POINTS), F32),
         name="pick_points",
     )(point_index.reshape(1, POINTS), orbitals)
 
@@ -111,24 +111,18 @@
         f_ref[...] = jnp.zeros_like(f_ref)
         for g in range(STEPS):
             f_ref[pl.ds(g, 1), :] = weight_ref[pl.ds(table_ref[kpoint, points[g]], 1), :]
-        p_ref[96:, :] = jnp.zeros((DEPTH - 96, POINTS), F32)
         p_ref[0:16, :] = jnp.where(same, mine[...], theirs[...])
         p_ref[16:32, :] = jnp.where(same, theirs[...], mine[...])
         for n in range(4):
             p_ref[32 + 16 * n : 48 + 16 * n, :] = before[n][...]
         for j in range(POINTS // 128):
             cols = slice(j * 128, (j + 1) * 128)
-            scaled = jnp.concatenate(
-                [p_ref[32 * g : 32 * g + 32, cols] * f_ref[g : g + 1, cols] for g in range(STEPS)] + [p_ref[96:, cols]], axis=0
-            )
-            high, low = split(scaled.T)
-            pt_ref[cols, 0:128] = high
-            pt_ref[cols, 128:256] = high
-            pt_ref[cols, 256:384] = low
+            scaled = jnp.concatenate([p_ref[32 * g : 32 * g + 32, cols] * f_ref[g : g + 1, cols] for g in range(STEPS)], axis=0)
+            high = scaled.astype(BF16).astype(F32)
+            pt_ref[cols, :] = jnp.concatenate([high, high, (scaled - high)[0:64]], axis=0).T.astype(BF16)
 
     row = lax.broadcasted_iota(jnp.int32, (32, 128), 0)
     number = jnp.where(row < 16, band, band ^ 1) * 8 + (row & 7)
-    fill = [jnp.zeros((DEPTH - 96, 128), F32)]
     sides = []
     for j in range(WIDE):
         here = pl.ds(pl.multiple_of((2 * (pl.program_id(0) * WIDE + j) + c) * 128, 128), 128)
@@ -139,9 +133,9 @@
             value = jnp.where(live, p_ref[32 * g : 32 * g + 32, here] * f_here[g : g + 1], 0.0)
             plain.append(value)
             turned += [value[8:16], -value[0:8], value[24:32], -value[16:24]]
-        sides += [jnp.concatenate(plain + fill, axis=0), jnp.concatenate(turned + fill, axis=0)]
+        sides += [jnp.concatenate(plain, axis=0), jnp.concatenate(turned, axis=0)]
     high, low = split(jnp.concatenate(sides, axis=1))
-    w = jnp.concatenate([high, low, high], axis=0)
+    w = jnp.concatenate([high, low, high[0:64]], axis=0)
     for n in range(POINTS // CHUNK):
         rows = slice(n * CHUNK, (n + 1) * CHUNK)
         e = jnp.dot(pt_ref[rows, :], w, preferred_element_type=F32)
@@ -169,8 +163,8 @@
             + [WHOLE] * 6,
             out_specs=[WHOLE, WHOLE],
             scratch_shapes=[
-                pltpu.VMEM((DEPTH, POINTS), F32),
-                pltpu.VMEM((POINTS, 3 * DEPTH), BF16),
+                pltpu.VMEM((32 * STEPS, POINTS), F32),
+                pltpu.VMEM((POINTS, DEPTH), BF16),
                 pltpu.VMEM((8, POINTS), F32),
             ],
         ),
@@ -230,7 +224,7 @@
         total_kernel,
         out_shape=jax.ShapeDtypeStruct((KPTS, 8, 2, 128), F32),
         name="total",
-    )(parts)
+    )(pltpu.with_memory_space_constraint(parts, pltpu.VMEM))
 
 
 def body(orbitals, point_index, kernel, q_weight, q_table, occ_count):
@@ -242,6 +236,7 @@
     far = [send(block, gather_pairs(1, t)) for t in range(2)]
     near = [send(block, gather_pairs(0, t)) for t in range(2)]
     before = [send(block, own_band_pairs()), send(block, next_band_pairs())]
+    before[0], before[1], near[0] = lax.optimization_barrier((before[0], before[1], near[0]))
     before_theirs = [send(value, core_pairs()) for value in before]
     near_theirs = [send(value, core_pairs()) for value in near]
     high, low = product(core, q_table, occ_count, q_weight, kernel, near[0], near_theirs[0], before + before_theirs)

time: 58.2 us -> 55.2 us (0.948)
  waiting for transfers between devices: 2.58 us -> 5.72 us
  blocking collectives: 22.6 us -> 19.7 us
  Pallas kernels: 14.8 us -> 12 us
    ppermute x12, waiting for transfers between devices: 2.58 us -> 5.72 us  [send(): return lax.ppermute(value, ('i', 'core', 'band'), pairs)]
    all_to_all x1, blocking collectives: 22.6 us -> 19.7 us  [body(): lax.all_to_all(parts.reshape(64, 2, 8, 128), ('i', 'band'), 0, 0, tiled=T...]
    pallas_call x1, Pallas kernels: 7.58 us -> 6.36 us  [product(): pl.pallas_call(product_kernel, grid_spec=pltpu.PrefetchScalarGridSpec(num...]
    pallas_call x1, Pallas kernels: 1.79 us -> 0.75 us  [total(): pl.pallas_call(total_kernel, out_shape=jax.ShapeDtypeStruct((KPTS, 8, 2,...]
    pallas_call x1, Pallas kernels: 1.92 us -> 1.24 us  [pick(): pl.pallas_call(pick_kernel, out_shape=pltpu.VMEM((ROWS, POINTS), F32), na...]
  transfers between devices with their start and end apart: 12 -> 12, of which waited for: 3 -> 5; matrix products, arithmetic and copies ran while one was open for 0% -> 0% of each run, Pallas kernels for 13% -> 12%
where the time goes in v3:
time: 55.2 us; the launch traced here: 55 us
  blocking collectives  19.7 us (36%)
  starting transfers between devices  17.4 us (32%)
  Pallas kernels  12 us (22%)
  waiting for transfers between devices  5.72 us (10%)
    all_to_all x1, blocking collectives, body(): lax.all_to_all(parts.reshape(64, 2, 8, 128), ('i', 'band'), 0, 0, tiled=T...  19.7 us
    ppermute x12, starting transfers between devices, send(): return lax.ppermute(value, ('i', 'core', 'band'), pairs)  17.4 us
    pallas_call x1, Pallas kernels, product(): pl.pallas_call(product_kernel, grid_spec=pltpu.PrefetchScalarGridSpec(num...  6.36 us
    ppermute x12, waiting for transfers between devices, send(): return lax.ppermute(value, ('i', 'core', 'band'), pairs)  5.72 us
    pallas_call x1, Pallas kernels, apply(): pl.pallas_call(apply_kernel, in_specs=[WHOLE] * 10, out_specs=WHOLE, out_...  3.69 us
    pallas_call x1, Pallas kernels, pick(): pl.pallas_call(pick_kernel, out_shape=pltpu.VMEM((ROWS, POINTS), F32), na...  1.24 us
  transfers between devices with their start and end apart: 12, of which 5 were waited for; matrix products, arithmetic and copies ran while one was open for 0% of the time, Pallas kernels for 12%

profile of v3, /device:TPU:0, one launch (start us, length us, event | category | flops | bytes accessed | tf_op | source)
XLA Modules:
  0.0 55.0 jit_solution(8162588122047730318)
XLA Ops:
  0.0 1.2 %pick_points.1 = f32[16,2048]{1,0:T(8,128)S(1)} custom-call(s32[1,2048]{1,0:T(1,128)} %bitcast.6, f32[8,2,4096]{2,1,0:T(2,128)} %bitcast.5), custom_call_target="tpu_custom_call" | custom-call | tf_op jit(solution)/shard_map/pick_points/pallas_call | solution.py:86
  1.2 0.7 %collective-permute-start.4 = (f32[16,2048]{1,0:T(8,128)S(1)}, f32[16,2048]{1,0:T(8,128)S(1)}, u32[]{:S(2)}, u32[]{:S(2)}) collective-permute-start(f32[16,2048]{1,0:T(8,128)S(1)} %pick_points.1), channel_id=1, source_target_pairs={{0,0},{1,8},{2,2},{3,10},{4,4},{5,12},{6,6},{7,14},{8,1},{9,9},{10... | collective-permute-start | bytes 393224 | tf_op jit(solution)/shard_map/ppermute | solution.py:62
  1.9 3.0 %collective-permute-start.3 = (f32[16,2048]{1,0:T(8,128)S(1)}, f32[16,2048]{1,0:T(8,128)S(1)}, u32[]{:S(2)}, u32[]{:S(2)}) collective-permute-start(f32[16,2048]{1,0:T(8,128)S(1)} %pick_points.1), channel_id=1, source_target_pairs={{0,1},{1,16},{2,3},{3,18},{4,5},{5,20},{6,7},{7,22},{8,25},{9,24},... | collective-permute-start | bytes 393224 | tf_op jit(solution)/shard_map/ppermute | solution.py:62
  4.9 3.4 %collective-permute-start.2 = (f32[16,2048]{1,0:T(8,128)S(1)}, f32[16,2048]{1,0:T(8,128)S(1)}, u32[]{:S(2)}, u32[]{:S(2)}) collective-permute-start(f32[16,2048]{1,0:T(8,128)S(1)} %pick_points.1), channel_id=1, source_target_pairs={{0,16},{1,1},{2,18},{3,3},{4,20},{5,5},{6,22},{7,7},{8,24},{9,25},... | collective-permute-start | bytes 393224 | tf_op jit(solution)/shard_map/ppermute | solution.py:62
  8.3 3.2 %collective-permute-start.8 = (f32[16,2048]{1,0:T(8,128)S(1)}, f32[16,2048]{1,0:T(8,128)S(1)}, u32[]{:S(2)}, u32[]{:S(2)}) collective-permute-start(f32[16,2048]{1,0:T(8,128)S(1)} %pick_points.1), channel_id=1, source_target_pairs={{0,2},{1,10},{2,0},{3,8},{4,6},{5,14},{6,4},{7,12},{8,3},{9,11},{1... | collective-permute-start | bytes 393224 | tf_op jit(solution)/shard_map/ppermute | solution.py:62
  11.5 0.0 collective-permute-done.4.refs_2_.refs_0_
  11.5 1.1 %collective-permute-done.3.refs_5_ = f32[16,2048]{1,0:T(8,128)S(1)} collective-permute-done((f32[16,2048]{1,0:T(8,128)S(1)}, f32[16,2048]{1,0:T(8,128)S(1)}, u32[]{:S(2)}, u32[]{:S(2)}) %collective-permute-start.3) | collective-permute-done | bytes 131104 | tf_op jit(solution)/shard_map/ppermute | solution.py:62
  12.6 3.0 %collective-permute-done.2.refs_4_ = f32[16,2048]{1,0:T(8,128)S(1)} collective-permute-done((f32[16,2048]{1,0:T(8,128)S(1)}, f32[16,2048]{1,0:T(8,128)S(1)}, u32[]{:S(2)}, u32[]{:S(2)}) %collective-permute-start.2) | collective-permute-done | bytes 131104 | tf_op jit(solution)/shard_map/ppermute | solution.py:62
  15.6 0.0 collective-permute-start.6
  15.6 0.5 collective-permute-start.7
  16.1 0.0 collective-permute-start.5
  16.1 6.1 %collective-permute-start.1 = (f32[16,2048]{1,0:T(8,128)S(1)}, f32[16,2048]{1,0:T(8,128)S(1)}, u32[]{:S(2)}, u32[]{:S(2)}) collective-permute-start(f32[16,2048]{1,0:T(8,128)S(1)} %pick_points.1), channel_id=1, source_target_pairs={{0,6},{1,14},{2,4},{3,12},{4,2},{5,10},{6,0},{7,8},{8,7},{9,15},{1... | collective-permute-start | bytes 393224 | tf_op jit(solution)/shard_map/ppermute | solution.py:62
  22.2 0.0 collective-permute-done.8.refs_1_
  22.2 0.0 collective-permute-start
  22.2 0.0 collective-permute-done.6.refs_6_
  22.2 0.1 collective-permute-start.9
  22.3 0.0 collective-permute-done.7.refs_7_
  22.3 0.0 collective-permute-done.5.refs_3_.refs_4_
  22.3 6.4 %kernel_product.1 = (bf16[4,2048,512]{2,1,0:T(8,128)(2,1)S(1)}, bf16[4,2048,512]{2,1,0:T(8,128)(2,1)S(1)}) custom-call(s32[1]{0:T(128)} %bitcast.2.core_ref, s32[16,16]{1,0:T(8,128)} %table_ref.1, s32[16]{0:T(128)} %occ_ref.1, f32[16,2048]{1,0:T(8,128)} %weight_ref.1, bf16[2048,2048]{1,0:T(8,128)(2,1)} %refs_1_.1, bf16[2048,2048]{1,0:T(8,128)(2,1)} %refs_1_.1, ...), custom_call_target="tpu_custom_call" | custom-call | flops 7000000000 | bytes 8388608 | tf_op jit(solution)/shard_map/kernel_product/pallas_call | solution.py:156
  28.7 0.0 collective-permute-done.1.refs_3_
  28.7 0.5 collective-permute-done.refs_2_
  29.3 0.0 collective-permute-start.10
  29.3 0.5 collective-permute-start.11
  29.8 0.0 collective-permute-done.9.refs_5_
  29.8 0.8 %collective-permute-done.10.refs_6_ = f32[16,2048]{1,0:T(8,128)S(1)} collective-permute-done((f32[16,2048]{1,0:T(8,128)S(1)}, f32[16,2048]{1,0:T(8,128)S(1)}, u32[]{:S(2)}, u32[]{:S(2)}) %collective-permute-start.10) | collective-permute-done | bytes 131104 | tf_op jit(solution)/shard_map/ppermute | solution.py:62
  30.6 0.2 collective-permute-done.11.refs_7_
  30.8 3.7 %apply_orbitals.1 = f32[8,8,2,8,128]{4,3,2,1,0:T(8,128)S(1)} custom-call(bf16[4,2048,512]{2,1,0:T(8,128)(2,1)S(1)} %get-tuple-element.19.high_ref, bf16[4,2048,512]{2,1,0:T(8,128)(2,1)S(1)} %get-tuple-element.20.low_ref, f32[16,2048]{1,0:T(8,128)S(1)} %collective-permute-done.4.refs_2_.refs_0_, f32[16,2048]{1,0:T(8,128)S(1)} %collective-permute-done.8.refs_1_, ...), custom_call_target="tpu_custom_call" | custom-call | flops 4000000000 | bytes 18874368 | tf_op jit(solution)/shard_map/apply_orbitals/pallas_call | solution.py:202
  34.5 19.7 %all_to_all.5.in_ref = f32[64,2,8,128]{3,2,1,0:T(8,128)S(1)} all-to-all(f32[64,2,8,128]{3,2,1,0:T(8,128)S(1)} %bitcast.4), channel_id=1, replica_groups=mesh['i'=8,'core'=2,'band'=8] {'i','band'}, dimensions={0} | all-to-all | bytes 1048576 | tf_op jit(solution)/shard_map/all_to_all | solution.py:246
  54.2 0.7 %total.1 = f32[16,8,2,128]{3,2,1,0:T(2,128)} custom-call(f32[64,2,8,128]{3,2,1,0:T(8,128)S(1)} %all_to_all.5.in_ref), custom_call_target="tpu_custom_call" | custom-call | tf_op jit(solution)/shard_map/total/pallas_call | solution.py:223
Async XLA Ops:
  1.2 10.2 %collective-permute-start.4 = (f32[16,2048]{1,0:T(8,128)S(1)}, f32[16,2048]{1,0:T(8,128)S(1)}, u32[]{:S(2)}, u32[]{:S(2)}) collective-permute-start(f32[16,2048]{1,0:T(8,128)S(1)} %pick_points.1), channel_id=1, source_target_pairs={{0,0},{1,8},{2,2},{3,10},{4,4},{5,12},{6,6},{7,14},{8,1},{9,9},{10... | collective-permute-start | bytes 393224 | tf_op jit(solution)/shard_map/ppermute | solution.py:62
  1.9 10.7 %collective-permute-start.3 = (f32[16,2048]{1,0:T(8,128)S(1)}, f32[16,2048]{1,0:T(8,128)S(1)}, u32[]{:S(2)}, u32[]{:S(2)}) collective-permute-start(f32[16,2048]{1,0:T(8,128)S(1)} %pick_points.1), channel_id=1, source_target_pairs={{0,1},{1,16},{2,3},{3,18},{4,5},{5,20},{6,7},{7,22},{8,25},{9,24},... | collective-permute-start | bytes 393224 | tf_op jit(solution)/shard_map/ppermute | solution.py:62
  4.9 10.7 %collective-permute-start.2 = (f32[16,2048]{1,0:T(8,128)S(1)}, f32[16,2048]{1,0:T(8,128)S(1)}, u32[]{:S(2)}, u32[]{:S(2)}) collective-permute-start(f32[16,2048]{1,0:T(8,128)S(1)} %pick_points.1), channel_id=1, source_target_pairs={{0,16},{1,1},{2,18},{3,3},{4,20},{5,5},{6,22},{7,7},{8,24},{9,25},... | collective-permute-start | bytes 393224 | tf_op jit(solution)/shard_map/ppermute | solution.py:62
  8.3 13.9 %collective-permute-start.8 = (f32[16,2048]{1,0:T(8,128)S(1)}, f32[16,2048]{1,0:T(8,128)S(1)}, u32[]{:S(2)}, u32[]{:S(2)}) collective-permute-start(f32[16,2048]{1,0:T(8,128)S(1)} %pick_points.1), channel_id=1, source_target_pairs={{0,2},{1,10},{2,0},{3,8},{4,6},{5,14},{6,4},{7,12},{8,3},{9,11},{1... | collective-permute-start | bytes 393224 | tf_op jit(solution)/shard_map/ppermute | solution.py:62
  15.6 6.6 %collective-permute-start.6 = (f32[16,2048]{1,0:T(8,128)S(1)}, f32[16,2048]{1,0:T(8,128)S(1)}, u32[]{:S(2)}, u32[]{:S(2)}) collective-permute-start(f32[16,2048]{1,0:T(8,128)S(1)} %collective-permute-done.2.refs_4_), channel_id=1, source_target_pairs={{0,8},{1,9},{2,10},{3,11},{4,12},{5,13},{6,14},{7,15},{8,0},{9,1},... | collective-permute-start | bytes 393224 | tf_op jit(solution)/shard_map/ppermute | solution.py:62
  15.6 6.7 %collective-permute-start.7 = (f32[16,2048]{1,0:T(8,128)S(1)}, f32[16,2048]{1,0:T(8,128)S(1)}, u32[]{:S(2)}, u32[]{:S(2)}) collective-permute-start(f32[16,2048]{1,0:T(8,128)S(1)} %collective-permute-done.3.refs_5_), channel_id=1, source_target_pairs={{0,8},{1,9},{2,10},{3,11},{4,12},{5,13},{6,14},{7,15},{8,0},{9,1},... | collective-permute-start | bytes 393224 | tf_op jit(solution)/shard_map/ppermute | solution.py:62
  16.1 6.2 %collective-permute-start.5 = (f32[16,2048]{1,0:T(8,128)S(1)}, f32[16,2048]{1,0:T(8,128)S(1)}, u32[]{:S(2)}, u32[]{:S(2)}) collective-permute-start(f32[16,2048]{1,0:T(8,128)S(1)} %collective-permute-done.4.refs_2_.refs_0_), channel_id=1, source_target_pairs={{0,8},{1,9},{2,10},{3,11},{4,12},{5,13},{6,14},{7,15},{8,0},{9,1},... | collective-permute-start | bytes 393224 | tf_op jit(solution)/shard_map/ppermute | solution.py:62
  16.1 12.6 %collective-permute-start.1 = (f32[16,2048]{1,0:T(8,128)S(1)}, f32[16,2048]{1,0:T(8,128)S(1)}, u32[]{:S(2)}, u32[]{:S(2)}) collective-permute-start(f32[16,2048]{1,0:T(8,128)S(1)} %pick_points.1), channel_id=1, source_target_pairs={{0,6},{1,14},{2,4},{3,12},{4,2},{5,10},{6,0},{7,8},{8,7},{9,15},{1... | collective-permute-start | bytes 393224 | tf_op jit(solution)/shard_map/ppermute | solution.py:62
  22.2 7.0 %collective-permute-start = (f32[16,2048]{1,0:T(8,128)S(1)}, f32[16,2048]{1,0:T(8,128)S(1)}, u32[]{:S(2)}, u32[]{:S(2)}) collective-permute-start(f32[16,2048]{1,0:T(8,128)S(1)} %pick_points.1), channel_id=1, source_target_pairs={{0,4},{1,12},{2,6},{3,14},{4,0},{5,8},{6,2},{7,10},{8,5},{9,13},{1... | collective-permute-start | bytes 393224 | tf_op jit(solution)/shard_map/ppermute | solution.py:62
  22.2 7.5 %collective-permute-start.9 = (f32[16,2048]{1,0:T(8,128)S(1)}, f32[16,2048]{1,0:T(8,128)S(1)}, u32[]{:S(2)}, u32[]{:S(2)}) collective-permute-start(f32[16,2048]{1,0:T(8,128)S(1)} %collective-permute-done.8.refs_1_), channel_id=1, source_target_pairs={{0,8},{1,9},{2,10},{3,11},{4,12},{5,13},{6,14},{7,15},{8,0},{9,1},... | collective-permute-start | bytes 393224 | tf_op jit(solution)/shard_map/ppermute | solution.py:62
  29.3 1.3 %collective-permute-start.10 = (f32[16,2048]{1,0:T(8,128)S(1)}, f32[16,2048]{1,0:T(8,128)S(1)}, u32[]{:S(2)}, u32[]{:S(2)}) collective-permute-start(f32[16,2048]{1,0:T(8,128)S(1)} %collective-permute-done.refs_2_), channel_id=1, source_target_pairs={{0,8},{1,9},{2,10},{3,11},{4,12},{5,13},{6,14},{7,15},{8,0},{9,1},... | collective-permute-start | bytes 393224 | tf_op jit(solution)/shard_map/ppermute | solution.py:62
  29.3 1.5 %collective-permute-start.11 = (f32[16,2048]{1,0:T(8,128)S(1)}, f32[16,2048]{1,0:T(8,128)S(1)}, u32[]{:S(2)}, u32[]{:S(2)}) collective-permute-start(f32[16,2048]{1,0:T(8,128)S(1)} %collective-permute-done.1.refs_3_), channel_id=1, source_target_pairs={{0,8},{1,9},{2,10},{3,11},{4,12},{5,13},{6,14},{7,15},{8,0},{9,1},... | collective-permute-start | bytes 393224 | tf_op jit(solution)/shard_map/ppermute | solution.py:62

commit v4 on v3

--- a/solution.py
+++ b/solution.py
@@ -236,7 +236,6 @@
     far = [send(block, gather_pairs(1, t)) for t in range(2)]
     near = [send(block, gather_pairs(0, t)) for t in range(2)]
     before = [send(block, own_band_pairs()), send(block, next_band_pairs())]
-    before[0], before[1], near[0] = lax.optimization_barrier((before[0], before[1], near[0]))
     before_theirs = [send(value, core_pairs()) for value in before]
     near_theirs = [send(value, core_pairs()) for value in near]
     high, low = product(core, q_table, occ_count, q_weight, kernel, near[0], near_theirs[0], before + before_theirs)

time: 55.2 us -> 54.7 us (level)
  waiting for transfers between devices: 5.72 us -> 3.45 us
  blocking collectives: 19.7 us -> 21.1 us
    ppermute x12, waiting for transfers between devices: 5.72 us -> 3.45 us  [send(): return lax.ppermute(value, ('i', 'core', 'band'), pairs)]
    all_to_all x1, blocking collectives: 19.7 us -> 21.1 us  [body(): lax.all_to_all(parts.reshape(64, 2, 8, 128), ('i', 'band'), 0, 0, tiled=T...]
  transfers between devices with their start and end apart: 12 -> 12, of which waited for: 5 -> 4; matrix products, arithmetic and copies ran while one was open for 0% -> 0% of each run, Pallas kernels for 12% -> 12%
where the time goes in v4:
time: 54.7 us; the launch traced here: 54.4 us
  blocking collectives  21.1 us (39%)
  starting transfers between devices  17.8 us (33%)
  Pallas kernels  12 us (22%)
  waiting for transfers between devices  3.45 us (6%)
    all_to_all x1, blocking collectives, body(): lax.all_to_all(parts.reshape(64, 2, 8, 128), ('i', 'band'), 0, 0, tiled=T...  21.1 us
    ppermute x12, starting transfers between devices, send(): return lax.ppermute(value, ('i', 'core', 'band'), pairs)  17.8 us
    pallas_call x1, Pallas kernels, product(): pl.pallas_call(product_kernel, grid_spec=pltpu.PrefetchScalarGridSpec(num...  6.36 us
    pallas_call x1, Pallas kernels, apply(): pl.pallas_call(apply_kernel, in_specs=[WHOLE] * 10, out_specs=WHOLE, out_...  3.69 us
    ppermute x12, waiting for transfers between devices, send(): return lax.ppermute(value, ('i', 'core', 'band'), pairs)  3.45 us
    pallas_call x1, Pallas kernels, pick(): pl.pallas_call(pick_kernel, out_shape=pltpu.VMEM((ROWS, POINTS), F32), na...  1.24 us
  transfers between devices with their start and end apart: 12, of which 4 were waited for; matrix products, arithmetic and copies ran while one was open for 0% of the time, Pallas kernels for 12%

profile of v4, /device:TPU:0, one launch (start us, length us, event | category | flops | bytes accessed | tf_op | source)
XLA Modules:
  0.0 54.4 jit_solution(11353800038637262834)
XLA Ops:
  0.0 1.2 %pick_points.1 = f32[16,2048]{1,0:T(8,128)S(1)} custom-call(s32[1,2048]{1,0:T(1,128)} %bitcast.6, f32[8,2,4096]{2,1,0:T(2,128)} %bitcast.5), custom_call_target="tpu_custom_call" | custom-call | tf_op jit(solution)/shard_map/pick_points/pallas_call | solution.py:86
  1.2 1.7 %collective-permute-start.5 = (f32[16,2048]{1,0:T(8,128)S(1)}, f32[16,2048]{1,0:T(8,128)S(1)}, u32[]{:S(2)}, u32[]{:S(2)}) collective-permute-start(f32[16,2048]{1,0:T(8,128)S(1)} %pick_points.1), channel_id=1, source_target_pairs={{0,1},{1,16},{2,3},{3,18},{4,5},{5,20},{6,7},{7,22},{8,25},{9,24},... | collective-permute-start | bytes 393224 | tf_op jit(solution)/shard_map/ppermute | solution.py:62
  3.0 3.4 %collective-permute-start.4 = (f32[16,2048]{1,0:T(8,128)S(1)}, f32[16,2048]{1,0:T(8,128)S(1)}, u32[]{:S(2)}, u32[]{:S(2)}) collective-permute-start(f32[16,2048]{1,0:T(8,128)S(1)} %pick_points.1), channel_id=1, source_target_pairs={{0,16},{1,1},{2,18},{3,3},{4,20},{5,5},{6,22},{7,7},{8,24},{9,25},... | collective-permute-start | bytes 393224 | tf_op jit(solution)/shard_map/ppermute | solution.py:62
  6.4 0.7 %collective-permute-start.2 = (f32[16,2048]{1,0:T(8,128)S(1)}, f32[16,2048]{1,0:T(8,128)S(1)}, u32[]{:S(2)}, u32[]{:S(2)}) collective-permute-start(f32[16,2048]{1,0:T(8,128)S(1)} %pick_points.1), channel_id=1, source_target_pairs={{0,0},{1,8},{2,2},{3,10},{4,4},{5,12},{6,6},{7,14},{8,1},{9,9},{10... | collective-permute-start | bytes 393224 | tf_op jit(solution)/shard_map/ppermute | solution.py:62
  7.0 3.0 %collective-permute-start.8 = (f32[16,2048]{1,0:T(8,128)S(1)}, f32[16,2048]{1,0:T(8,128)S(1)}, u32[]{:S(2)}, u32[]{:S(2)}) collective-permute-start(f32[16,2048]{1,0:T(8,128)S(1)} %pick_points.1), channel_id=1, source_target_pairs={{0,2},{1,10},{2,0},{3,8},{4,6},{5,14},{6,4},{7,12},{8,3},{9,11},{1... | collective-permute-start | bytes 393224 | tf_op jit(solution)/shard_map/ppermute | solution.py:62
  10.0 0.0 collective-permute-done.5.refs_5_
  10.0 1.7 %collective-permute-start.7 = (f32[16,2048]{1,0:T(8,128)S(1)}, f32[16,2048]{1,0:T(8,128)S(1)}, u32[]{:S(2)}, u32[]{:S(2)}) collective-permute-start(f32[16,2048]{1,0:T(8,128)S(1)} %collective-permute-done.5.refs_5_), channel_id=1, source_target_pairs={{0,8},{1,9},{2,10},{3,11},{4,12},{5,13},{6,14},{7,15},{8,0},{9,1},... | collective-permute-start | bytes 393224 | tf_op jit(solution)/shard_map/ppermute | solution.py:62
  11.8 1.1 %collective-permute-done.4.refs_4_ = f32[16,2048]{1,0:T(8,128)S(1)} collective-permute-done((f32[16,2048]{1,0:T(8,128)S(1)}, f32[16,2048]{1,0:T(8,128)S(1)}, u32[]{:S(2)}, u32[]{:S(2)}) %collective-permute-start.4) | collective-permute-done | bytes 131104 | tf_op jit(solution)/shard_map/ppermute | solution.py:62
  12.9 0.0 collective-permute-start.6
  12.9 0.0 collective-permute-done.2.refs_2_.refs_0_
  12.9 1.0 %collective-permute-start.3 = (f32[16,2048]{1,0:T(8,128)S(1)}, f32[16,2048]{1,0:T(8,128)S(1)}, u32[]{:S(2)}, u32[]{:S(2)}) collective-permute-start(f32[16,2048]{1,0:T(8,128)S(1)} %collective-permute-done.2.refs_2_.refs_0_), channel_id=1, source_target_pairs={{0,8},{1,9},{2,10},{3,11},{4,12},{5,13},{6,14},{7,15},{8,0},{9,1},... | collective-permute-start | bytes 393224 | tf_op jit(solution)/shard_map/ppermute | solution.py:62
  13.9 5.7 %collective-permute-start.1 = (f32[16,2048]{1,0:T(8,128)S(1)}, f32[16,2048]{1,0:T(8,128)S(1)}, u32[]{:S(2)}, u32[]{:S(2)}) collective-permute-start(f32[16,2048]{1,0:T(8,128)S(1)} %pick_points.1), channel_id=1, source_target_pairs={{0,6},{1,14},{2,4},{3,12},{4,2},{5,10},{6,0},{7,8},{8,7},{9,15},{1... | collective-permute-start | bytes 393224 | tf_op jit(solution)/shard_map/ppermute | solution.py:62
  19.6 0.0 collective-permute-done.8.refs_1_
  19.6 0.0 collective-permute-start
  19.6 0.0 collective-permute-done.7.refs_7_
  19.6 0.1 collective-permute-start.9
  19.7 0.0 collective-permute-done.6.refs_6_
  19.7 0.0 collective-permute-done.3.refs_3_.refs_4_
  19.7 6.4 %kernel_product.1 = (bf16[4,2048,512]{2,1,0:T(8,128)(2,1)S(1)}, bf16[4,2048,512]{2,1,0:T(8,128)(2,1)S(1)}) custom-call(s32[1]{0:T(128)} %bitcast.2.core_ref, s32[16,16]{1,0:T(8,128)} %table_ref.1, s32[16]{0:T(128)} %occ_ref.1, f32[16,2048]{1,0:T(8,128)} %weight_ref.1, bf16[2048,2048]{1,0:T(8,128)(2,1)} %refs_1_.1, bf16[2048,2048]{1,0:T(8,128)(2,1)} %refs_1_.1, ...), custom_call_target="tpu_custom_call" | custom-call | flops 7000000000 | bytes 8388608 | tf_op jit(solution)/shard_map/kernel_product/pallas_call | solution.py:156
  26.1 0.0 collective-permute-done.1.refs_3_
  26.1 1.3 %collective-permute-done.refs_2_ = f32[16,2048]{1,0:T(8,128)S(1)} collective-permute-done((f32[16,2048]{1,0:T(8,128)S(1)}, f32[16,2048]{1,0:T(8,128)S(1)}, u32[]{:S(2)}, u32[]{:S(2)}) %collective-permute-start) | collective-permute-done | bytes 131104 | tf_op jit(solution)/shard_map/ppermute | solution.py:62
  27.4 0.0 collective-permute-start.10
  27.4 0.5 collective-permute-start.11
  27.9 0.0 collective-permute-done.9.refs_5_
  27.9 0.8 %collective-permute-done.10.refs_6_ = f32[16,2048]{1,0:T(8,128)S(1)} collective-permute-done((f32[16,2048]{1,0:T(8,128)S(1)}, f32[16,2048]{1,0:T(8,128)S(1)}, u32[]{:S(2)}, u32[]{:S(2)}) %collective-permute-start.10) | collective-permute-done | bytes 131104 | tf_op jit(solution)/shard_map/ppermute | solution.py:62
  28.7 0.2 collective-permute-done.11.refs_7_
  28.9 3.7 %apply_orbitals.1 = f32[8,8,2,8,128]{4,3,2,1,0:T(8,128)S(1)} custom-call(bf16[4,2048,512]{2,1,0:T(8,128)(2,1)S(1)} %get-tuple-element.13.high_ref, bf16[4,2048,512]{2,1,0:T(8,128)(2,1)S(1)} %get-tuple-element.14.low_ref, f32[16,2048]{1,0:T(8,128)S(1)} %collective-permute-done.2.refs_2_.refs_0_, f32[16,2048]{1,0:T(8,128)S(1)} %collective-permute-done.8.refs_1_, ...), custom_call_target="tpu_custom_call" | custom-call | flops 4000000000 | bytes 18874368 | tf_op jit(solution)/shard_map/apply_orbitals/pallas_call | solution.py:202
  32.6 21.1 %all_to_all.5.in_ref = f32[64,2,8,128]{3,2,1,0:T(8,128)S(1)} all-to-all(f32[64,2,8,128]{3,2,1,0:T(8,128)S(1)} %bitcast.4), channel_id=1, replica_groups=mesh['i'=8,'core'=2,'band'=8] {'i','band'}, dimensions={0} | all-to-all | bytes 1048576 | tf_op jit(solution)/shard_map/all_to_all | solution.py:245
  53.7 0.7 %total.1 = f32[16,8,2,128]{3,2,1,0:T(2,128)} custom-call(f32[64,2,8,128]{3,2,1,0:T(8,128)S(1)} %all_to_all.5.in_ref), custom_call_target="tpu_custom_call" | custom-call | tf_op jit(solution)/shard_map/total/pallas_call | solution.py:223
Async XLA Ops:
  1.2 8.8 %collective-permute-start.5 = (f32[16,2048]{1,0:T(8,128)S(1)}, f32[16,2048]{1,0:T(8,128)S(1)}, u32[]{:S(2)}, u32[]{:S(2)}) collective-permute-start(f32[16,2048]{1,0:T(8,128)S(1)} %pick_points.1), channel_id=1, source_target_pairs={{0,1},{1,16},{2,3},{3,18},{4,5},{5,20},{6,7},{7,22},{8,25},{9,24},... | collective-permute-start | bytes 393224 | tf_op jit(solution)/shard_map/ppermute | solution.py:62
  3.0 9.9 %collective-permute-start.4 = (f32[16,2048]{1,0:T(8,128)S(1)}, f32[16,2048]{1,0:T(8,128)S(1)}, u32[]{:S(2)}, u32[]{:S(2)}) collective-permute-start(f32[16,2048]{1,0:T(8,128)S(1)} %pick_points.1), channel_id=1, source_target_pairs={{0,16},{1,1},{2,18},{3,3},{4,20},{5,5},{6,22},{7,7},{8,24},{9,25},... | collective-permute-start | bytes 393224 | tf_op jit(solution)/shard_map/ppermute | solution.py:62
  6.4 6.5 %collective-permute-start.2 = (f32[16,2048]{1,0:T(8,128)S(1)}, f32[16,2048]{1,0:T(8,128)S(1)}, u32[]{:S(2)}, u32[]{:S(2)}) collective-permute-start(f32[16,2048]{1,0:T(8,128)S(1)} %pick_points.1), channel_id=1, source_target_pairs={{0,0},{1,8},{2,2},{3,10},{4,4},{5,12},{6,6},{7,14},{8,1},{9,9},{10... | collective-permute-start | bytes 393224 | tf_op jit(solution)/shard_map/ppermute | solution.py:62
  7.0 12.5 %collective-permute-start.8 = (f32[16,2048]{1,0:T(8,128)S(1)}, f32[16,2048]{1,0:T(8,128)S(1)}, u32[]{:S(2)}, u32[]{:S(2)}) collective-permute-start(f32[16,2048]{1,0:T(8,128)S(1)} %pick_points.1), channel_id=1, source_target_pairs={{0,2},{1,10},{2,0},{3,8},{4,6},{5,14},{6,4},{7,12},{8,3},{9,11},{1... | collective-permute-start | bytes 393224 | tf_op jit(solution)/shard_map/ppermute | solution.py:62
  10.0 9.5 %collective-permute-start.7 = (f32[16,2048]{1,0:T(8,128)S(1)}, f32[16,2048]{1,0:T(8,128)S(1)}, u32[]{:S(2)}, u32[]{:S(2)}) collective-permute-start(f32[16,2048]{1,0:T(8,128)S(1)} %collective-permute-done.5.refs_5_), channel_id=1, source_target_pairs={{0,8},{1,9},{2,10},{3,11},{4,12},{5,13},{6,14},{7,15},{8,0},{9,1},... | collective-permute-start | bytes 393224 | tf_op jit(solution)/shard_map/ppermute | solution.py:62
  12.9 6.8 %collective-permute-start.6 = (f32[16,2048]{1,0:T(8,128)S(1)}, f32[16,2048]{1,0:T(8,128)S(1)}, u32[]{:S(2)}, u32[]{:S(2)}) collective-permute-start(f32[16,2048]{1,0:T(8,128)S(1)} %collective-permute-done.4.refs_4_), channel_id=1, source_target_pairs={{0,8},{1,9},{2,10},{3,11},{4,12},{5,13},{6,14},{7,15},{8,0},{9,1},... | collective-permute-start | bytes 393224 | tf_op jit(solution)/shard_map/ppermute | solution.py:62
  12.9 6.8 %collective-permute-start.3 = (f32[16,2048]{1,0:T(8,128)S(1)}, f32[16,2048]{1,0:T(8,128)S(1)}, u32[]{:S(2)}, u32[]{:S(2)}) collective-permute-start(f32[16,2048]{1,0:T(8,128)S(1)} %collective-permute-done.2.refs_2_.refs_0_), channel_id=1, source_target_pairs={{0,8},{1,9},{2,10},{3,11},{4,12},{5,13},{6,14},{7,15},{8,0},{9,1},... | collective-permute-start | bytes 393224 | tf_op jit(solution)/shard_map/ppermute | solution.py:62
  13.9 12.2 %collective-permute-start.1 = (f32[16,2048]{1,0:T(8,128)S(1)}, f32[16,2048]{1,0:T(8,128)S(1)}, u32[]{:S(2)}, u32[]{:S(2)}) collective-permute-start(f32[16,2048]{1,0:T(8,128)S(1)} %pick_points.1), channel_id=1, source_target_pairs={{0,6},{1,14},{2,4},{3,12},{4,2},{5,10},{6,0},{7,8},{8,7},{9,15},{1... | collective-permute-start | bytes 393224 | tf_op jit(solution)/shard_map/ppermute | solution.py:62
  19.6 7.8 %collective-permute-start = (f32[16,2048]{1,0:T(8,128)S(1)}, f32[16,2048]{1,0:T(8,128)S(1)}, u32[]{:S(2)}, u32[]{:S(2)}) collective-permute-start(f32[16,2048]{1,0:T(8,128)S(1)} %pick_points.1), channel_id=1, source_target_pairs={{0,4},{1,12},{2,6},{3,14},{4,0},{5,8},{6,2},{7,10},{8,5},{9,13},{1... | collective-permute-start | bytes 393224 | tf_op jit(solution)/shard_map/ppermute | solution.py:62
  19.6 8.3 %collective-permute-start.9 = (f32[16,2048]{1,0:T(8,128)S(1)}, f32[16,2048]{1,0:T(8,128)S(1)}, u32[]{:S(2)}, u32[]{:S(2)}) collective-permute-start(f32[16,2048]{1,0:T(8,128)S(1)} %collective-permute-done.8.refs_1_), channel_id=1, source_target_pairs={{0,8},{1,9},{2,10},{3,11},{4,12},{5,13},{6,14},{7,15},{8,0},{9,1},... | collective-permute-start | bytes 393224 | tf_op jit(solution)/shard_map/ppermute | solution.py:62
  27.4 1.3 %collective-permute-start.10 = (f32[16,2048]{1,0:T(8,128)S(1)}, f32[16,2048]{1,0:T(8,128)S(1)}, u32[]{:S(2)}, u32[]{:S(2)}) collective-permute-start(f32[16,2048]{1,0:T(8,128)S(1)} %collective-permute-done.refs_2_), channel_id=1, source_target_pairs={{0,8},{1,9},{2,10},{3,11},{4,12},{5,13},{6,14},{7,15},{8,0},{9,1},... | collective-permute-start | bytes 393224 | tf_op jit(solution)/shard_map/ppermute | solution.py:62
  27.4 1.5 %collective-permute-start.11 = (f32[16,2048]{1,0:T(8,128)S(1)}, f32[16,2048]{1,0:T(8,128)S(1)}, u32[]{:S(2)}, u32[]{:S(2)}) collective-permute-start(f32[16,2048]{1,0:T(8,128)S(1)} %collective-permute-done.1.refs_3_), channel_id=1, source_target_pairs={{0,8},{1,9},{2,10},{3,11},{4,12},{5,13},{6,14},{7,15},{8,0},{9,1},... | collective-permute-start | bytes 393224 | tf_op jit(solution)/shard_map/ppermute | solution.py:62

commit v5 on v4

--- a/solution.py
+++ b/solution.py
@@ -233,13 +233,13 @@
         pltpu.with_memory_space_constraint(value, pltpu.HBM) for value in (kernel, q_weight, q_table, occ_count)
     )
     block = pick(orbitals[0], point_index)
-    far = [send(block, gather_pairs(1, t)) for t in range(2)]
+    far = [send(block, gather_pairs(1, t)) for t in (1, 0)][::-1]
     near = [send(block, gather_pairs(0, t)) for t in range(2)]
     before = [send(block, own_band_pairs()), send(block, next_band_pairs())]
     before_theirs = [send(value, core_pairs()) for value in before]
     near_theirs = [send(value, core_pairs()) for value in near]
     high, low = product(core, q_table, occ_count, q_weight, kernel, near[0], near_theirs[0], before + before_theirs)
-    far[0], far[1], high, low = lax.optimization_barrier((far[0], far[1], high, low))
+    far[1], high, low = lax.optimization_barrier((far[1], high, low))
     far_theirs = [send(value, core_pairs()) for value in far]
     parts = apply(high, low, near + far, near_theirs + far_theirs)
     got = lax.all_to_all(parts.reshape(64, 2, 8, 128), ("i", "band"), 0, 0, tiled=True)

time: 54.7 us -> 54.3 us (level)
  blocking collectives: 21.1 us -> 19.7 us
  waiting for transfers between devices: 3.45 us -> 4.14 us
    all_to_all x1, blocking collectives: 21.1 us -> 19.7 us  [body(): lax.all_to_all(parts.reshape(64, 2, 8, 128), ('i', 'band'), 0, 0, tiled=T...]
    ppermute x12, waiting for transfers between devices: 3.45 us -> 4.14 us  [send(): return lax.ppermute(value, ('i', 'core', 'band'), pairs)]
  transfers between devices with their start and end apart: 12 -> 12, of which waited for: 4 -> 2; matrix products, arithmetic and copies ran while one was open for 0% -> 0% of each run, Pallas kernels for 12% -> 12%
where the time goes in v5:
time: 54.3 us; the launch traced here: 54.1 us
  blocking collectives  19.7 us (36%)
  starting transfers between devices  18.1 us (33%)
  Pallas kernels  12 us (22%)
  waiting for transfers between devices  4.14 us (8%)
    all_to_all x1, blocking collectives, body(): lax.all_to_all(parts.reshape(64, 2, 8, 128), ('i', 'band'), 0, 0, tiled=T...  19.7 us
    ppermute x12, starting transfers between devices, send(): return lax.ppermute(value, ('i', 'core', 'band'), pairs)  18.1 us
    pallas_call x1, Pallas kernels, product(): pl.pallas_call(product_kernel, grid_spec=pltpu.PrefetchScalarGridSpec(num...  6.34 us
    ppermute x12, waiting for transfers between devices, send(): return lax.ppermute(value, ('i', 'core', 'band'), pairs)  4.14 us
    pallas_call x1, Pallas kernels, apply(): pl.pallas_call(apply_kernel, in_specs=[WHOLE] * 10, out_specs=WHOLE, out_...  3.69 us
    pallas_call x1, Pallas kernels, pick(): pl.pallas_call(pick_kernel, out_shape=pltpu.VMEM((ROWS, POINTS), F32), na...  1.24 us
  transfers between devices with their start and end apart: 12, of which 2 were waited for; matrix products, arithmetic and copies ran while one was open for 0% of the time, Pallas kernels for 12%

profile of v5, /device:TPU:0, one launch (start us, length us, event | category | flops | bytes accessed | tf_op | source)
XLA Modules:
  0.0 54.1 jit_solution(14880048759008797654)
XLA Ops:
  0.0 1.2 %pick_points.1 = f32[16,2048]{1,0:T(8,128)S(1)} custom-call(s32[1,2048]{1,0:T(1,128)} %bitcast.6, f32[8,2,4096]{2,1,0:T(2,128)} %bitcast.5), custom_call_target="tpu_custom_call" | custom-call | tf_op jit(solution)/shard_map/pick_points/pallas_call | solution.py:86
  1.2 1.7 %collective-permute-start.4 = (f32[16,2048]{1,0:T(8,128)S(1)}, f32[16,2048]{1,0:T(8,128)S(1)}, u32[]{:S(2)}, u32[]{:S(2)}) collective-permute-start(f32[16,2048]{1,0:T(8,128)S(1)} %pick_points.1), channel_id=1, source_target_pairs={{0,1},{1,16},{2,3},{3,18},{4,5},{5,20},{6,7},{7,22},{8,25},{9,24},... | collective-permute-start | bytes 393224 | tf_op jit(solution)/shard_map/ppermute | solution.py:62
  3.0 3.4 %collective-permute-start.3 = (f32[16,2048]{1,0:T(8,128)S(1)}, f32[16,2048]{1,0:T(8,128)S(1)}, u32[]{:S(2)}, u32[]{:S(2)}) collective-permute-start(f32[16,2048]{1,0:T(8,128)S(1)} %pick_points.1), channel_id=1, source_target_pairs={{0,16},{1,1},{2,18},{3,3},{4,20},{5,5},{6,22},{7,7},{8,24},{9,25},... | collective-permute-start | bytes 393224 | tf_op jit(solution)/shard_map/ppermute | solution.py:62
  6.4 0.7 %collective-permute-start.1 = (f32[16,2048]{1,0:T(8,128)S(1)}, f32[16,2048]{1,0:T(8,128)S(1)}, u32[]{:S(2)}, u32[]{:S(2)}) collective-permute-start(f32[16,2048]{1,0:T(8,128)S(1)} %pick_points.1), channel_id=1, source_target_pairs={{0,0},{1,8},{2,2},{3,10},{4,4},{5,12},{6,6},{7,14},{8,1},{9,9},{10... | collective-permute-start | bytes 393224 | tf_op jit(solution)/shard_map/ppermute | solution.py:62
  7.0 4.0 %collective-permute-start.8 = (f32[16,2048]{1,0:T(8,128)S(1)}, f32[16,2048]{1,0:T(8,128)S(1)}, u32[]{:S(2)}, u32[]{:S(2)}) collective-permute-start(f32[16,2048]{1,0:T(8,128)S(1)} %pick_points.1), channel_id=1, source_target_pairs={{0,4},{1,12},{2,6},{3,14},{4,0},{5,8},{6,2},{7,10},{8,5},{9,13},{1... | collective-permute-start | bytes 393224 | tf_op jit(solution)/shard_map/ppermute | solution.py:62
  11.0 2.9 %collective-permute-start.7 = (f32[16,2048]{1,0:T(8,128)S(1)}, f32[16,2048]{1,0:T(8,128)S(1)}, u32[]{:S(2)}, u32[]{:S(2)}) collective-permute-start(f32[16,2048]{1,0:T(8,128)S(1)} %pick_points.1), channel_id=1, source_target_pairs={{0,2},{1,10},{2,0},{3,8},{4,6},{5,14},{6,4},{7,12},{8,3},{9,11},{1... | collective-permute-start | bytes 393224 | tf_op jit(solution)/shard_map/ppermute | solution.py:62
  13.9 0.0 collective-permute-done.4.refs_5_
  13.9 1.2 %collective-permute-start.6 = (f32[16,2048]{1,0:T(8,128)S(1)}, f32[16,2048]{1,0:T(8,128)S(1)}, u32[]{:S(2)}, u32[]{:S(2)}) collective-permute-start(f32[16,2048]{1,0:T(8,128)S(1)} %collective-permute-done.4.refs_5_), channel_id=1, source_target_pairs={{0,8},{1,9},{2,10},{3,11},{4,12},{5,13},{6,14},{7,15},{8,0},{9,1},... | collective-permute-start | bytes 393224 | tf_op jit(solution)/shard_map/ppermute | solution.py:62
  15.1 0.0 collective-permute-done.3.refs_4_
  15.1 0.1 collective-permute-start.5
  15.2 0.0 collective-permute-done.1.refs_2_.refs_0_
  15.2 0.4 collective-permute-start.2
  15.6 3.1 %collective-permute-done.8.refs_2_ = f32[16,2048]{1,0:T(8,128)S(1)} collective-permute-done((f32[16,2048]{1,0:T(8,128)S(1)}, f32[16,2048]{1,0:T(8,128)S(1)}, u32[]{:S(2)}, u32[]{:S(2)}) %collective-permute-start.8) | collective-permute-done | bytes 131104 | tf_op jit(solution)/shard_map/ppermute | solution.py:62
  18.7 2.2 %collective-permute-start = (f32[16,2048]{1,0:T(8,128)S(1)}, f32[16,2048]{1,0:T(8,128)S(1)}, u32[]{:S(2)}, u32[]{:S(2)}) collective-permute-start(f32[16,2048]{1,0:T(8,128)S(1)} %pick_points.1), channel_id=1, source_target_pairs={{0,6},{1,14},{2,4},{3,12},{4,2},{5,10},{6,0},{7,8},{8,7},{9,15},{1... | collective-permute-start | bytes 393224 | tf_op jit(solution)/shard_map/ppermute | solution.py:62
  20.9 0.0 collective-permute-done.7.refs_1_
  20.9 1.1 %collective-permute-start.10 = (f32[16,2048]{1,0:T(8,128)S(1)}, f32[16,2048]{1,0:T(8,128)S(1)}, u32[]{:S(2)}, u32[]{:S(2)}) collective-permute-start(f32[16,2048]{1,0:T(8,128)S(1)} %collective-permute-done.8.refs_2_), channel_id=1, source_target_pairs={{0,8},{1,9},{2,10},{3,11},{4,12},{5,13},{6,14},{7,15},{8,0},{9,1},... | collective-permute-start | bytes 393224 | tf_op jit(solution)/shard_map/ppermute | solution.py:62
  22.0 0.0 collective-permute-done.6.refs_7_
  22.0 0.1 collective-permute-start.9
  22.1 0.0 collective-permute-done.5.refs_6_
  22.1 0.0 collective-permute-done.2.refs_3_.refs_4_
  22.1 6.3 %kernel_product.1 = (bf16[4,2048,512]{2,1,0:T(8,128)(2,1)S(1)}, bf16[4,2048,512]{2,1,0:T(8,128)(2,1)S(1)}) custom-call(s32[1]{0:T(128)} %bitcast.2.core_ref, s32[16,16]{1,0:T(8,128)} %table_ref.1, s32[16]{0:T(128)} %occ_ref.1, f32[16,2048]{1,0:T(8,128)} %weight_ref.1, bf16[2048,2048]{1,0:T(8,128)(2,1)} %refs_1_.1, bf16[2048,2048]{1,0:T(8,128)(2,1)} %refs_1_.1, ...), custom_call_target="tpu_custom_call" | custom-call | flops 7000000000 | bytes 8388608 | tf_op jit(solution)/shard_map/kernel_product/pallas_call | solution.py:156
  28.4 0.0 collective-permute-done.refs_3_
  28.4 0.5 collective-permute-start.11
  28.9 0.0 collective-permute-done.10.refs_6_
  28.9 0.0 collective-permute-done.9.refs_5_
  28.9 1.0 %collective-permute-done.11.refs_7_ = f32[16,2048]{1,0:T(8,128)S(1)} collective-permute-done((f32[16,2048]{1,0:T(8,128)S(1)}, f32[16,2048]{1,0:T(8,128)S(1)}, u32[]{:S(2)}, u32[]{:S(2)}) %collective-permute-start.11) | collective-permute-done | bytes 131104 | tf_op jit(solution)/shard_map/ppermute | solution.py:62
  29.9 3.7 %apply_orbitals.1 = f32[8,8,2,8,128]{4,3,2,1,0:T(8,128)S(1)} custom-call(bf16[4,2048,512]{2,1,0:T(8,128)(2,1)S(1)} %get-tuple-element.12.high_ref, bf16[4,2048,512]{2,1,0:T(8,128)(2,1)S(1)} %get-tuple-element.13.low_ref, f32[16,2048]{1,0:T(8,128)S(1)} %collective-permute-done.1.refs_2_.refs_0_, f32[16,2048]{1,0:T(8,128)S(1)} %collective-permute-done.7.refs_1_, ...), custom_call_target="tpu_custom_call" | custom-call | flops 4000000000 | bytes 18874368 | tf_op jit(solution)/shard_map/apply_orbitals/pallas_call | solution.py:202
  33.6 19.7 %all_to_all.5.in_ref = f32[64,2,8,128]{3,2,1,0:T(8,128)S(1)} all-to-all(f32[64,2,8,128]{3,2,1,0:T(8,128)S(1)} %bitcast.4), channel_id=1, replica_groups=mesh['i'=8,'core'=2,'band'=8] {'i','band'}, dimensions={0} | all-to-all | bytes 1048576 | tf_op jit(solution)/shard_map/all_to_all | solution.py:245
  53.3 0.7 %total.1 = f32[16,8,2,128]{3,2,1,0:T(2,128)} custom-call(f32[64,2,8,128]{3,2,1,0:T(8,128)S(1)} %all_to_all.5.in_ref), custom_call_target="tpu_custom_call" | custom-call | tf_op jit(solution)/shard_map/total/pallas_call | solution.py:223
Async XLA Ops:
  1.2 12.7 %collective-permute-start.4 = (f32[16,2048]{1,0:T(8,128)S(1)}, f32[16,2048]{1,0:T(8,128)S(1)}, u32[]{:S(2)}, u32[]{:S(2)}) collective-permute-start(f32[16,2048]{1,0:T(8,128)S(1)} %pick_points.1), channel_id=1, source_target_pairs={{0,1},{1,16},{2,3},{3,18},{4,5},{5,20},{6,7},{7,22},{8,25},{9,24},... | collective-permute-start | bytes 393224 | tf_op jit(solution)/shard_map/ppermute | solution.py:62
  3.0 12.1 %collective-permute-start.3 = (f32[16,2048]{1,0:T(8,128)S(1)}, f32[16,2048]{1,0:T(8,128)S(1)}, u32[]{:S(2)}, u32[]{:S(2)}) collective-permute-start(f32[16,2048]{1,0:T(8,128)S(1)} %pick_points.1), channel_id=1, source_target_pairs={{0,16},{1,1},{2,18},{3,3},{4,20},{5,5},{6,22},{7,7},{8,24},{9,25},... | collective-permute-start | bytes 393224 | tf_op jit(solution)/shard_map/ppermute | solution.py:62
  6.4 8.8 %collective-permute-start.1 = (f32[16,2048]{1,0:T(8,128)S(1)}, f32[16,2048]{1,0:T(8,128)S(1)}, u32[]{:S(2)}, u32[]{:S(2)}) collective-permute-start(f32[16,2048]{1,0:T(8,128)S(1)} %pick_points.1), channel_id=1, source_target_pairs={{0,0},{1,8},{2,2},{3,10},{4,4},{5,12},{6,6},{7,14},{8,1},{9,9},{10... | collective-permute-start | bytes 393224 | tf_op jit(solution)/shard_map/ppermute | solution.py:62
  7.0 11.7 %collective-permute-start.8 = (f32[16,2048]{1,0:T(8,128)S(1)}, f32[16,2048]{1,0:T(8,128)S(1)}, u32[]{:S(2)}, u32[]{:S(2)}) collective-permute-start(f32[16,2048]{1,0:T(8,128)S(1)} %pick_points.1), channel_id=1, source_target_pairs={{0,4},{1,12},{2,6},{3,14},{4,0},{5,8},{6,2},{7,10},{8,5},{9,13},{1... | collective-permute-start | bytes 393224 | tf_op jit(solution)/shard_map/ppermute | solution.py:62
  11.0 9.9 %collective-permute-start.7 = (f32[16,2048]{1,0:T(8,128)S(1)}, f32[16,2048]{1,0:T(8,128)S(1)}, u32[]{:S(2)}, u32[]{:S(2)}) collective-permute-start(f32[16,2048]{1,0:T(8,128)S(1)} %pick_points.1), channel_id=1, source_target_pairs={{0,2},{1,10},{2,0},{3,8},{4,6},{5,14},{6,4},{7,12},{8,3},{9,11},{1... | collective-permute-start | bytes 393224 | tf_op jit(solution)/shard_map/ppermute | solution.py:62
  13.9 8.1 %collective-permute-start.6 = (f32[16,2048]{1,0:T(8,128)S(1)}, f32[16,2048]{1,0:T(8,128)S(1)}, u32[]{:S(2)}, u32[]{:S(2)}) collective-permute-start(f32[16,2048]{1,0:T(8,128)S(1)} %collective-permute-done.4.refs_5_), channel_id=1, source_target_pairs={{0,8},{1,9},{2,10},{3,11},{4,12},{5,13},{6,14},{7,15},{8,0},{9,1},... | collective-permute-start | bytes 393224 | tf_op jit(solution)/shard_map/ppermute | solution.py:62
  15.1 7.0 %collective-permute-start.5 = (f32[16,2048]{1,0:T(8,128)S(1)}, f32[16,2048]{1,0:T(8,128)S(1)}, u32[]{:S(2)}, u32[]{:S(2)}) collective-permute-start(f32[16,2048]{1,0:T(8,128)S(1)} %collective-permute-done.3.refs_4_), channel_id=1, source_target_pairs={{0,8},{1,9},{2,10},{3,11},{4,12},{5,13},{6,14},{7,15},{8,0},{9,1},... | collective-permute-start | bytes 393224 | tf_op jit(solution)/shard_map/ppermute | solution.py:62
  15.2 6.9 %collective-permute-start.2 = (f32[16,2048]{1,0:T(8,128)S(1)}, f32[16,2048]{1,0:T(8,128)S(1)}, u32[]{:S(2)}, u32[]{:S(2)}) collective-permute-start(f32[16,2048]{1,0:T(8,128)S(1)} %collective-permute-done.1.refs_2_.refs_0_), channel_id=1, source_target_pairs={{0,8},{1,9},{2,10},{3,11},{4,12},{5,13},{6,14},{7,15},{8,0},{9,1},... | collective-permute-start | bytes 393224 | tf_op jit(solution)/shard_map/ppermute | solution.py:62
  18.7 9.7 %collective-permute-start = (f32[16,2048]{1,0:T(8,128)S(1)}, f32[16,2048]{1,0:T(8,128)S(1)}, u32[]{:S(2)}, u32[]{:S(2)}) collective-permute-start(f32[16,2048]{1,0:T(8,128)S(1)} %pick_points.1), channel_id=1, source_target_pairs={{0,6},{1,14},{2,4},{3,12},{4,2},{5,10},{6,0},{7,8},{8,7},{9,15},{1... | collective-permute-start | bytes 393224 | tf_op jit(solution)/shard_map/ppermute | solution.py:62
  20.9 8.0 %collective-permute-start.10 = (f32[16,2048]{1,0:T(8,128)S(1)}, f32[16,2048]{1,0:T(8,128)S(1)}, u32[]{:S(2)}, u32[]{:S(2)}) collective-permute-start(f32[16,2048]{1,0:T(8,128)S(1)} %collective-permute-done.8.refs_2_), channel_id=1, source_target_pairs={{0,8},{1,9},{2,10},{3,11},{4,12},{5,13},{6,14},{7,15},{8,0},{9,1},... | collective-permute-start | bytes 393224 | tf_op jit(solution)/shard_map/ppermute | solution.py:62
  22.0 7.0 %collective-permute-start.9 = (f32[16,2048]{1,0:T(8,128)S(1)}, f32[16,2048]{1,0:T(8,128)S(1)}, u32[]{:S(2)}, u32[]{:S(2)}) collective-permute-start(f32[16,2048]{1,0:T(8,128)S(1)} %collective-permute-done.7.refs_1_), channel_id=1, source_target_pairs={{0,8},{1,9},{2,10},{3,11},{4,12},{5,13},{6,14},{7,15},{8,0},{9,1},... | collective-permute-start | bytes 393224 | tf_op jit(solution)/shard_map/ppermute | solution.py:62
  28.4 1.5 %collective-permute-start.11 = (f32[16,2048]{1,0:T(8,128)S(1)}, f32[16,2048]{1,0:T(8,128)S(1)}, u32[]{:S(2)}, u32[]{:S(2)}) collective-permute-start(f32[16,2048]{1,0:T(8,128)S(1)} %collective-permute-done.refs_3_), channel_id=1, source_target_pairs={{0,8},{1,9},{2,10},{3,11},{4,12},{5,13},{6,14},{7,15},{8,0},{9,1},... | collective-permute-start | bytes 393224 | tf_op jit(solution)/shard_map/ppermute | solution.py:62

commit v6 on v5

--- a/solution.py
+++ b/solution.py
@@ -95,7 +95,7 @@
     return high, (value - high.astype(F32)).astype(BF16)
 
 
-def product_kernel(core_ref, table_ref, occ_ref, weight_ref, *refs):
+def product_kernel(table_ref, occ_ref, weight_ref, *refs):
     k_refs, refs = refs[:WIDE], refs[WIDE:]
     mine, theirs, before = refs[0], refs[1], refs[2:6]
     high_ref, low_ref, p_ref, pt_ref, f_ref = refs[6:]
@@ -152,14 +152,14 @@
 SMEM = pl.BlockSpec(memory_space=pltpu.SMEM)
 
 
-def product(core, q_table, occ_count, q_weight, kernel, mine, theirs, before):
+def product(q_table, occ_count, q_weight, kernel, mine, theirs, before):
     return pl.pallas_call(
         product_kernel,
         grid_spec=pltpu.PrefetchScalarGridSpec(
-            num_scalar_prefetch=1,
+            num_scalar_prefetch=0,
             grid=(TILES,),
             in_specs=[SMEM, SMEM, WHOLE]
-            + [pl.BlockSpec((POINTS, 128), lambda u, core, j=j: (0, 2 * (u * WIDE + j) + core[0])) for j in range(WIDE)]
+            + [pl.BlockSpec((POINTS, 128), lambda u, j=j: (0, 2 * (u * WIDE + j) + lax.axis_index("core"))) for j in range(WIDE)]
             + [WHOLE] * 6,
             out_specs=[WHOLE, WHOLE],
             scratch_shapes=[
@@ -172,7 +172,7 @@
         compiler_params=pltpu.CompilerParams(vmem_limit_bytes=28 * 2**20),
         cost_estimate=pl.CostEstimate(flops=7 * 10**9, bytes_accessed=8 * 2**20, transcendentals=0),
         name="kernel_product",
-    )(core, q_table, occ_count, q_weight, *[kernel] * WIDE, mine, theirs, *before)
+    )(q_table, occ_count, q_weight, *[kernel] * WIDE, mine, theirs, *before)
 
 
 def apply_kernel(high_ref, low_ref, *refs):
@@ -228,7 +228,6 @@
 
 
 def body(orbitals, point_index, kernel, q_weight, q_table, occ_count):
-    core = lax.axis_index("core").astype(jnp.int32).reshape(1)
     kernel, q_weight, q_table, occ_count = (
         pltpu.with_memory_space_constraint(value, pltpu.HBM) for value in (kernel, q_weight, q_table, occ_count)
     )
@@ -238,7 +237,7 @@
     before = [send(block, own_band_pairs()), send(block, next_band_pairs())]
     before_theirs = [send(value, core_pairs()) for value in before]
     near_theirs = [send(value, core_pairs()) for value in near]
-    high, low = product(core, q_table, occ_count, q_weight, kernel, near[0], near_theirs[0], before + before_theirs)
+    high, low = product(q_table, occ_count, q_weight, kernel, near[0], near_theirs[0], before + before_theirs)
     far[1], high, low = lax.optimization_barrier((far[1], high, low))
     far_theirs = [send(value, core_pairs()) for value in far]
     parts = apply(high, low, near + far, near_theirs + far_theirs)

time: 54.3 us -> 54.3 us (level)
  no operation moved by 1% of the time
where the time goes in v6:
time: 54.3 us; the launch traced here: 54 us
  blocking collectives  19.7 us (36%)
  starting transfers between devices  18.1 us (33%)
  Pallas kernels  11.9 us (22%)
  waiting for transfers between devices  4.14 us (8%)
    all_to_all x1, blocking collectives, body(): lax.all_to_all(parts.reshape(64, 2, 8, 128), ('i', 'band'), 0, 0, tiled=T...  19.7 us
    ppermute x12, starting transfers between devices, send(): return lax.ppermute(value, ('i', 'core', 'band'), pairs)  18.1 us
    pallas_call x1, Pallas kernels, product(): pl.pallas_call(product_kernel, grid_spec=pltpu.PrefetchScalarGridSpec(num...  6.41 us
    ppermute x12, waiting for transfers between devices, send(): return lax.ppermute(value, ('i', 'core', 'band'), pairs)  4.14 us
    pallas_call x1, Pallas kernels, apply(): pl.pallas_call(apply_kernel, in_specs=[WHOLE] * 10, out_specs=WHOLE, out_...  3.54 us
    pallas_call x1, Pallas kernels, pick(): pl.pallas_call(pick_kernel, out_shape=pltpu.VMEM((ROWS, POINTS), F32), na...  1.24 us
  transfers between devices with their start and end apart: 12, of which 2 were waited for; matrix products, arithmetic and copies ran while one was open for 0% of the time, Pallas kernels for 12%

profile of v6, /device:TPU:0, one launch (start us, length us, event | category | flops | bytes accessed | tf_op | source)
XLA Modules:
  0.0 54.0 jit_solution(11008936805011260213)
XLA Ops:
  0.0 1.2 %pick_points.1 = f32[16,2048]{1,0:T(8,128)S(1)} custom-call(s32[1,2048]{1,0:T(1,128)} %bitcast.5, f32[8,2,4096]{2,1,0:T(2,128)} %bitcast.4), custom_call_target="tpu_custom_call" | custom-call | tf_op jit(solution)/shard_map/pick_points/pallas_call | solution.py:86
  1.2 1.7 %collective-permute-start.4 = (f32[16,2048]{1,0:T(8,128)S(1)}, f32[16,2048]{1,0:T(8,128)S(1)}, u32[]{:S(2)}, u32[]{:S(2)}) collective-permute-start(f32[16,2048]{1,0:T(8,128)S(1)} %pick_points.1), channel_id=1, source_target_pairs={{0,1},{1,16},{2,3},{3,18},{4,5},{5,20},{6,7},{7,22},{8,25},{9,24},... | collective-permute-start | bytes 393224 | tf_op jit(solution)/shard_map/ppermute | solution.py:62
  3.0 3.4 %collective-permute-start.3 = (f32[16,2048]{1,0:T(8,128)S(1)}, f32[16,2048]{1,0:T(8,128)S(1)}, u32[]{:S(2)}, u32[]{:S(2)}) collective-permute-start(f32[16,2048]{1,0:T(8,128)S(1)} %pick_points.1), channel_id=1, source_target_pairs={{0,16},{1,1},{2,18},{3,3},{4,20},{5,5},{6,22},{7,7},{8,24},{9,25},... | collective-permute-start | bytes 393224 | tf_op jit(solution)/shard_map/ppermute | solution.py:62
  6.4 0.7 %collective-permute-start.1 = (f32[16,2048]{1,0:T(8,128)S(1)}, f32[16,2048]{1,0:T(8,128)S(1)}, u32[]{:S(2)}, u32[]{:S(2)}) collective-permute-start(f32[16,2048]{1,0:T(8,128)S(1)} %pick_points.1), channel_id=1, source_target_pairs={{0,0},{1,8},{2,2},{3,10},{4,4},{5,12},{6,6},{7,14},{8,1},{9,9},{10... | collective-permute-start | bytes 393224 | tf_op jit(solution)/shard_map/ppermute | solution.py:62
  7.0 4.0 %collective-permute-start.8 = (f32[16,2048]{1,0:T(8,128)S(1)}, f32[16,2048]{1,0:T(8,128)S(1)}, u32[]{:S(2)}, u32[]{:S(2)}) collective-permute-start(f32[16,2048]{1,0:T(8,128)S(1)} %pick_points.1), channel_id=1, source_target_pairs={{0,4},{1,12},{2,6},{3,14},{4,0},{5,8},{6,2},{7,10},{8,5},{9,13},{1... | collective-permute-start | bytes 393224 | tf_op jit(solution)/shard_map/ppermute | solution.py:62
  11.0 2.9 %collective-permute-start.7 = (f32[16,2048]{1,0:T(8,128)S(1)}, f32[16,2048]{1,0:T(8,128)S(1)}, u32[]{:S(2)}, u32[]{:S(2)}) collective-permute-start(f32[16,2048]{1,0:T(8,128)S(1)} %pick_points.1), channel_id=1, source_target_pairs={{0,2},{1,10},{2,0},{3,8},{4,6},{5,14},{6,4},{7,12},{8,3},{9,11},{1... | collective-permute-start | bytes 393224 | tf_op jit(solution)/shard_map/ppermute | solution.py:62
  13.9 0.0 collective-permute-done.4.refs_5_
  13.9 1.2 %collective-permute-start.6 = (f32[16,2048]{1,0:T(8,128)S(1)}, f32[16,2048]{1,0:T(8,128)S(1)}, u32[]{:S(2)}, u32[]{:S(2)}) collective-permute-start(f32[16,2048]{1,0:T(8,128)S(1)} %collective-permute-done.4.refs_5_), channel_id=1, source_target_pairs={{0,8},{1,9},{2,10},{3,11},{4,12},{5,13},{6,14},{7,15},{8,0},{9,1},... | collective-permute-start | bytes 393224 | tf_op jit(solution)/shard_map/ppermute | solution.py:62
  15.1 0.0 collective-permute-done.3.refs_4_
  15.1 0.1 collective-permute-start.5
  15.2 0.0 collective-permute-done.1.refs_2_.refs_0_
  15.2 0.4 collective-permute-start.2
  15.6 3.1 %collective-permute-done.8.refs_2_ = f32[16,2048]{1,0:T(8,128)S(1)} collective-permute-done((f32[16,2048]{1,0:T(8,128)S(1)}, f32[16,2048]{1,0:T(8,128)S(1)}, u32[]{:S(2)}, u32[]{:S(2)}) %collective-permute-start.8) | collective-permute-done | bytes 131104 | tf_op jit(solution)/shard_map/ppermute | solution.py:62
  18.7 2.2 %collective-permute-start = (f32[16,2048]{1,0:T(8,128)S(1)}, f32[16,2048]{1,0:T(8,128)S(1)}, u32[]{:S(2)}, u32[]{:S(2)}) collective-permute-start(f32[16,2048]{1,0:T(8,128)S(1)} %pick_points.1), channel_id=1, source_target_pairs={{0,6},{1,14},{2,4},{3,12},{4,2},{5,10},{6,0},{7,8},{8,7},{9,15},{1... | collective-permute-start | bytes 393224 | tf_op jit(solution)/shard_map/ppermute | solution.py:62
  20.9 0.0 collective-permute-done.7.refs_1_
  20.9 1.1 %collective-permute-start.10 = (f32[16,2048]{1,0:T(8,128)S(1)}, f32[16,2048]{1,0:T(8,128)S(1)}, u32[]{:S(2)}, u32[]{:S(2)}) collective-permute-start(f32[16,2048]{1,0:T(8,128)S(1)} %collective-permute-done.8.refs_2_), channel_id=1, source_target_pairs={{0,8},{1,9},{2,10},{3,11},{4,12},{5,13},{6,14},{7,15},{8,0},{9,1},... | collective-permute-start | bytes 393224 | tf_op jit(solution)/shard_map/ppermute | solution.py:62
  22.0 0.0 collective-permute-done.6.refs_7_
  22.0 0.1 collective-permute-start.9
  22.1 0.0 collective-permute-done.5.refs_6_
  22.1 0.0 collective-permute-done.2.refs_3_.refs_4_
  22.1 6.4 %kernel_product.1 = (bf16[4,2048,512]{2,1,0:T(8,128)(2,1)S(1)}, bf16[4,2048,512]{2,1,0:T(8,128)(2,1)S(1)}) custom-call(s32[16,16]{1,0:T(8,128)} %table_ref.1, s32[16]{0:T(128)} %occ_ref.1, f32[16,2048]{1,0:T(8,128)} %weight_ref.1, bf16[2048,2048]{1,0:T(8,128)(2,1)} %refs_1_.1, bf16[2048,2048]{1,0:T(8,128)(2,1)} %refs_1_.1, ...), custom_call_target="tpu_custom_call" | custom-call | flops 7000000000 | bytes 8388608 | tf_op jit(solution)/shard_map/kernel_product/pallas_call | solution.py:156
  28.5 0.0 collective-permute-done.refs_3_
  28.5 0.5 collective-permute-start.11
  29.0 0.0 collective-permute-done.10.refs_6_
  29.0 0.0 collective-permute-done.9.refs_5_
  29.0 1.0 %collective-permute-done.11.refs_7_ = f32[16,2048]{1,0:T(8,128)S(1)} collective-permute-done((f32[16,2048]{1,0:T(8,128)S(1)}, f32[16,2048]{1,0:T(8,128)S(1)}, u32[]{:S(2)}, u32[]{:S(2)}) %collective-permute-start.11) | collective-permute-done | bytes 131104 | tf_op jit(solution)/shard_map/ppermute | solution.py:62
  30.0 3.5 %apply_orbitals.1 = f32[8,8,2,8,128]{4,3,2,1,0:T(8,128)S(1)} custom-call(bf16[4,2048,512]{2,1,0:T(8,128)(2,1)S(1)} %get-tuple-element.12.high_ref, bf16[4,2048,512]{2,1,0:T(8,128)(2,1)S(1)} %get-tuple-element.13.low_ref, f32[16,2048]{1,0:T(8,128)S(1)} %collective-permute-done.1.refs_2_.refs_0_, f32[16,2048]{1,0:T(8,128)S(1)} %collective-permute-done.7.refs_1_, ...), custom_call_target="tpu_custom_call" | custom-call | flops 4000000000 | bytes 18874368 | tf_op jit(solution)/shard_map/apply_orbitals/pallas_call | solution.py:202
  33.5 19.7 %all_to_all.5.in_ref = f32[64,2,8,128]{3,2,1,0:T(8,128)S(1)} all-to-all(f32[64,2,8,128]{3,2,1,0:T(8,128)S(1)} %bitcast.3), channel_id=1, replica_groups=mesh['i'=8,'core'=2,'band'=8] {'i','band'}, dimensions={0} | all-to-all | bytes 1048576 | tf_op jit(solution)/shard_map/all_to_all | solution.py:244
  53.2 0.7 %total.1 = f32[16,8,2,128]{3,2,1,0:T(2,128)} custom-call(f32[64,2,8,128]{3,2,1,0:T(8,128)S(1)} %all_to_all.5.in_ref), custom_call_target="tpu_custom_call" | custom-call | tf_op jit(solution)/shard_map/total/pallas_call | solution.py:223
Async XLA Ops:
  1.2 12.7 %collective-permute-start.4 = (f32[16,2048]{1,0:T(8,128)S(1)}, f32[16,2048]{1,0:T(8,128)S(1)}, u32[]{:S(2)}, u32[]{:S(2)}) collective-permute-start(f32[16,2048]{1,0:T(8,128)S(1)} %pick_points.1), channel_id=1, source_target_pairs={{0,1},{1,16},{2,3},{3,18},{4,5},{5,20},{6,7},{7,22},{8,25},{9,24},... | collective-permute-start | bytes 393224 | tf_op jit(solution)/shard_map/ppermute | solution.py:62
  3.0 12.1 %collective-permute-start.3 = (f32[16,2048]{1,0:T(8,128)S(1)}, f32[16,2048]{1,0:T(8,128)S(1)}, u32[]{:S(2)}, u32[]{:S(2)}) collective-permute-start(f32[16,2048]{1,0:T(8,128)S(1)} %pick_points.1), channel_id=1, source_target_pairs={{0,16},{1,1},{2,18},{3,3},{4,20},{5,5},{6,22},{7,7},{8,24},{9,25},... | collective-permute-start | bytes 393224 | tf_op jit(solution)/shard_map/ppermute | solution.py:62
  6.4 8.8 %collective-permute-start.1 = (f32[16,2048]{1,0:T(8,128)S(1)}, f32[16,2048]{1,0:T(8,128)S(1)}, u32[]{:S(2)}, u32[]{:S(2)}) collective-permute-start(f32[16,2048]{1,0:T(8,128)S(1)} %pick_points.1), channel_id=1, source_target_pairs={{0,0},{1,8},{2,2},{3,10},{4,4},{5,12},{6,6},{7,14},{8,1},{9,9},{10... | collective-permute-start | bytes 393224 | tf_op jit(solution)/shard_map/ppermute | solution.py:62
  7.0 11.7 %collective-permute-start.8 = (f32[16,2048]{1,0:T(8,128)S(1)}, f32[16,2048]{1,0:T(8,128)S(1)}, u32[]{:S(2)}, u32[]{:S(2)}) collective-permute-start(f32[16,2048]{1,0:T(8,128)S(1)} %pick_points.1), channel_id=1, source_target_pairs={{0,4},{1,12},{2,6},{3,14},{4,0},{5,8},{6,2},{7,10},{8,5},{9,13},{1... | collective-permute-start | bytes 393224 | tf_op jit(solution)/shard_map/ppermute | solution.py:62
  11.0 9.9 %collective-permute-start.7 = (f32[16,2048]{1,0:T(8,128)S(1)}, f32[16,2048]{1,0:T(8,128)S(1)}, u32[]{:S(2)}, u32[]{:S(2)}) collective-permute-start(f32[16,2048]{1,0:T(8,128)S(1)} %pick_points.1), channel_id=1, source_target_pairs={{0,2},{1,10},{2,0},{3,8},{4,6},{5,14},{6,4},{7,12},{8,3},{9,11},{1... | collective-permute-start | bytes 393224 | tf_op jit(solution)/shard_map/ppermute | solution.py:62
  13.9 8.1 %collective-permute-start.6 = (f32[16,2048]{1,0:T(8,128)S(1)}, f32[16,2048]{1,0:T(8,128)S(1)}, u32[]{:S(2)}, u32[]{:S(2)}) collective-permute-start(f32[16,2048]{1,0:T(8,128)S(1)} %collective-permute-done.4.refs_5_), channel_id=1, source_target_pairs={{0,8},{1,9},{2,10},{3,11},{4,12},{5,13},{6,14},{7,15},{8,0},{9,1},... | collective-permute-start | bytes 393224 | tf_op jit(solution)/shard_map/ppermute | solution.py:62
  15.1 7.0 %collective-permute-start.5 = (f32[16,2048]{1,0:T(8,128)S(1)}, f32[16,2048]{1,0:T(8,128)S(1)}, u32[]{:S(2)}, u32[]{:S(2)}) collective-permute-start(f32[16,2048]{1,0:T(8,128)S(1)} %collective-permute-done.3.refs_4_), channel_id=1, source_target_pairs={{0,8},{1,9},{2,10},{3,11},{4,12},{5,13},{6,14},{7,15},{8,0},{9,1},... | collective-permute-start | bytes 393224 | tf_op jit(solution)/shard_map/ppermute | solution.py:62
  15.2 6.9 %collective-permute-start.2 = (f32[16,2048]{1,0:T(8,128)S(1)}, f32[16,2048]{1,0:T(8,128)S(1)}, u32[]{:S(2)}, u32[]{:S(2)}) collective-permute-start(f32[16,2048]{1,0:T(8,128)S(1)} %collective-permute-done.1.refs_2_.refs_0_), channel_id=1, source_target_pairs={{0,8},{1,9},{2,10},{3,11},{4,12},{5,13},{6,14},{7,15},{8,0},{9,1},... | collective-permute-start | bytes 393224 | tf_op jit(solution)/shard_map/ppermute | solution.py:62
  18.7 9.7 %collective-permute-start = (f32[16,2048]{1,0:T(8,128)S(1)}, f32[16,2048]{1,0:T(8,128)S(1)}, u32[]{:S(2)}, u32[]{:S(2)}) collective-permute-start(f32[16,2048]{1,0:T(8,128)S(1)} %pick_points.1), channel_id=1, source_target_pairs={{0,6},{1,14},{2,4},{3,12},{4,2},{5,10},{6,0},{7,8},{8,7},{9,15},{1... | collective-permute-start | bytes 393224 | tf_op jit(solution)/shard_map/ppermute | solution.py:62
  20.9 8.1 %collective-permute-start.10 = (f32[16,2048]{1,0:T(8,128)S(1)}, f32[16,2048]{1,0:T(8,128)S(1)}, u32[]{:S(2)}, u32[]{:S(2)}) collective-permute-start(f32[16,2048]{1,0:T(8,128)S(1)} %collective-permute-done.8.refs_2_), channel_id=1, source_target_pairs={{0,8},{1,9},{2,10},{3,11},{4,12},{5,13},{6,14},{7,15},{8,0},{9,1},... | collective-permute-start | bytes 393224 | tf_op jit(solution)/shard_map/ppermute | solution.py:62
  22.0 7.0 %collective-permute-start.9 = (f32[16,2048]{1,0:T(8,128)S(1)}, f32[16,2048]{1,0:T(8,128)S(1)}, u32[]{:S(2)}, u32[]{:S(2)}) collective-permute-start(f32[16,2048]{1,0:T(8,128)S(1)} %collective-permute-done.7.refs_1_), channel_id=1, source_target_pairs={{0,8},{1,9},{2,10},{3,11},{4,12},{5,13},{6,14},{7,15},{8,0},{9,1},... | collective-permute-start | bytes 393224 | tf_op jit(solution)/shard_map/ppermute | solution.py:62
  28.5 1.5 %collective-permute-start.11 = (f32[16,2048]{1,0:T(8,128)S(1)}, f32[16,2048]{1,0:T(8,128)S(1)}, u32[]{:S(2)}, u32[]{:S(2)}) collective-permute-start(f32[16,2048]{1,0:T(8,128)S(1)} %collective-permute-done.refs_3_), channel_id=1, source_target_pairs={{0,8},{1,9},{2,10},{3,11},{4,12},{5,13},{6,14},{7,15},{8,0},{9,1},... | collective-permute-start | bytes 393224 | tf_op jit(solution)/shard_map/ppermute | solution.py:62

commit v7 on v5

--- a/solution.py
+++ b/solution.py
@@ -14,7 +14,7 @@
 TILES = 4
 WIDE = 2
 DEPTH = 256
-CHUNK = 512
+CHUNK = 1024
 FACTOR = -1.0 / (STEPS * 64) ** 0.5
 F32, BF16 = jnp.float32, jnp.bfloat16
 
@@ -235,7 +235,7 @@
     block = pick(orbitals[0], point_index)
     far = [send(block, gather_pairs(1, t)) for t in (1, 0)][::-1]
     near = [send(block, gather_pairs(0, t)) for t in range(2)]
-    before = [send(block, own_band_pairs()), send(block, next_band_pairs())]
+    before = [send(block, pairs) for pairs in (next_band_pairs(), own_band_pairs())][::-1]
     before_theirs = [send(value, core_pairs()) for value in before]
     near_theirs = [send(value, core_pairs()) for value in near]
     high, low = product(core, q_table, occ_count, q_weight, kernel, near[0], near_theirs[0], before + before_theirs)

time: 54.3 us -> 54.3 us (level)
  no operation moved by 1% of the time
where the time goes in v7:
time: 54.3 us; the launch traced here: 54.1 us
  blocking collectives  19.7 us (36%)
  starting transfers between devices  18.1 us (33%)
  Pallas kernels  12 us (22%)
  waiting for transfers between devices  4.14 us (8%)
    all_to_all x1, blocking collectives, body(): lax.all_to_all(parts.reshape(64, 2, 8, 128), ('i', 'band'), 0, 0, tiled=T...  19.7 us
    ppermute x12, starting transfers between devices, send(): return lax.ppermute(value, ('i', 'core', 'band'), pairs)  18.1 us
    pallas_call x1, Pallas kernels, product(): pl.pallas_call(product_kernel, grid_spec=pltpu.PrefetchScalarGridSpec(num...  6.32 us
    ppermute x12, waiting for transfers between devices, send(): return lax.ppermute(value, ('i', 'core', 'band'), pairs)  4.14 us
    pallas_call x1, Pallas kernels, apply(): pl.pallas_call(apply_kernel, in_specs=[WHOLE] * 10, out_specs=WHOLE, out_...  3.69 us
    pallas_call x1, Pallas kernels, pick(): pl.pallas_call(pick_kernel, out_shape=pltpu.VMEM((ROWS, POINTS), F32), na...  1.24 us
  transfers between devices with their start and end apart: 12, of which 2 were waited for; matrix products, arithmetic and copies ran while one was open for 0% of the time, Pallas kernels for 12%

profile of v7, /device:TPU:0, one launch (start us, length us, event | category | flops | bytes accessed | tf_op | source)
XLA Modules:
  0.0 54.1 jit_solution(5242609041043313403)
XLA Ops:
  0.0 1.2 %pick_points.1 = f32[16,2048]{1,0:T(8,128)S(1)} custom-call(s32[1,2048]{1,0:T(1,128)} %bitcast.6, f32[8,2,4096]{2,1,0:T(2,128)} %bitcast.5), custom_call_target="tpu_custom_call" | custom-call | tf_op jit(solution)/shard_map/pick_points/pallas_call | solution.py:86
  1.2 1.7 %collective-permute-start.4 = (f32[16,2048]{1,0:T(8,128)S(1)}, f32[16,2048]{1,0:T(8,128)S(1)}, u32[]{:S(2)}, u32[]{:S(2)}) collective-permute-start(f32[16,2048]{1,0:T(8,128)S(1)} %pick_points.1), channel_id=1, source_target_pairs={{0,1},{1,16},{2,3},{3,18},{4,5},{5,20},{6,7},{7,22},{8,25},{9,24},... | collective-permute-start | bytes 393224 | tf_op jit(solution)/shard_map/ppermute | solution.py:62
  3.0 3.4 %collective-permute-start.3 = (f32[16,2048]{1,0:T(8,128)S(1)}, f32[16,2048]{1,0:T(8,128)S(1)}, u32[]{:S(2)}, u32[]{:S(2)}) collective-permute-start(f32[16,2048]{1,0:T(8,128)S(1)} %pick_points.1), channel_id=1, source_target_pairs={{0,16},{1,1},{2,18},{3,3},{4,20},{5,5},{6,22},{7,7},{8,24},{9,25},... | collective-permute-start | bytes 393224 | tf_op jit(solution)/shard_map/ppermute | solution.py:62
  6.4 0.7 %collective-permute-start.1 = (f32[16,2048]{1,0:T(8,128)S(1)}, f32[16,2048]{1,0:T(8,128)S(1)}, u32[]{:S(2)}, u32[]{:S(2)}) collective-permute-start(f32[16,2048]{1,0:T(8,128)S(1)} %pick_points.1), channel_id=1, source_target_pairs={{0,0},{1,8},{2,2},{3,10},{4,4},{5,12},{6,6},{7,14},{8,1},{9,9},{10... | collective-permute-start | bytes 393224 | tf_op jit(solution)/shard_map/ppermute | solution.py:62
  7.0 4.0 %collective-permute-start.8 = (f32[16,2048]{1,0:T(8,128)S(1)}, f32[16,2048]{1,0:T(8,128)S(1)}, u32[]{:S(2)}, u32[]{:S(2)}) collective-permute-start(f32[16,2048]{1,0:T(8,128)S(1)} %pick_points.1), channel_id=1, source_target_pairs={{0,4},{1,12},{2,6},{3,14},{4,0},{5,8},{6,2},{7,10},{8,5},{9,13},{1... | collective-permute-start | bytes 393224 | tf_op jit(solution)/shard_map/ppermute | solution.py:62
  11.0 2.9 %collective-permute-start.7 = (f32[16,2048]{1,0:T(8,128)S(1)}, f32[16,2048]{1,0:T(8,128)S(1)}, u32[]{:S(2)}, u32[]{:S(2)}) collective-permute-start(f32[16,2048]{1,0:T(8,128)S(1)} %pick_points.1), channel_id=1, source_target_pairs={{0,2},{1,10},{2,0},{3,8},{4,6},{5,14},{6,4},{7,12},{8,3},{9,11},{1... | collective-permute-start | bytes 393224 | tf_op jit(solution)/shard_map/ppermute | solution.py:62
  13.9 0.0 collective-permute-done.4.refs_5_
  13.9 1.2 %collective-permute-start.6 = (f32[16,2048]{1,0:T(8,128)S(1)}, f32[16,2048]{1,0:T(8,128)S(1)}, u32[]{:S(2)}, u32[]{:S(2)}) collective-permute-start(f32[16,2048]{1,0:T(8,128)S(1)} %collective-permute-done.4.refs_5_), channel_id=1, source_target_pairs={{0,8},{1,9},{2,10},{3,11},{4,12},{5,13},{6,14},{7,15},{8,0},{9,1},... | collective-permute-start | bytes 393224 | tf_op jit(solution)/shard_map/ppermute | solution.py:62
  15.1 0.0 collective-permute-done.3.refs_4_
  15.1 0.1 collective-permute-start.5
  15.2 0.0 collective-permute-done.1.refs_2_.refs_0_
  15.2 0.4 collective-permute-start.2
  15.6 3.1 %collective-permute-done.8.refs_2_ = f32[16,2048]{1,0:T(8,128)S(1)} collective-permute-done((f32[16,2048]{1,0:T(8,128)S(1)}, f32[16,2048]{1,0:T(8,128)S(1)}, u32[]{:S(2)}, u32[]{:S(2)}) %collective-permute-start.8) | collective-permute-done | bytes 131104 | tf_op jit(solution)/shard_map/ppermute | solution.py:62
  18.7 2.2 %collective-permute-start = (f32[16,2048]{1,0:T(8,128)S(1)}, f32[16,2048]{1,0:T(8,128)S(1)}, u32[]{:S(2)}, u32[]{:S(2)}) collective-permute-start(f32[16,2048]{1,0:T(8,128)S(1)} %pick_points.1), channel_id=1, source_target_pairs={{0,6},{1,14},{2,4},{3,12},{4,2},{5,10},{6,0},{7,8},{8,7},{9,15},{1... | collective-permute-start | bytes 393224 | tf_op jit(solution)/shard_map/ppermute | solution.py:62
  20.9 0.0 collective-permute-done.7.refs_1_
  20.9 1.1 %collective-permute-start.10 = (f32[16,2048]{1,0:T(8,128)S(1)}, f32[16,2048]{1,0:T(8,128)S(1)}, u32[]{:S(2)}, u32[]{:S(2)}) collective-permute-start(f32[16,2048]{1,0:T(8,128)S(1)} %collective-permute-done.8.refs_2_), channel_id=1, source_target_pairs={{0,8},{1,9},{2,10},{3,11},{4,12},{5,13},{6,14},{7,15},{8,0},{9,1},... | collective-permute-start | bytes 393224 | tf_op jit(solution)/shard_map/ppermute | solution.py:62
  22.0 0.0 collective-permute-done.6.refs_7_
  22.0 0.1 collective-permute-start.9
  22.1 0.0 collective-permute-done.5.refs_6_
  22.1 0.0 collective-permute-done.2.refs_3_.refs_4_
  22.1 6.3 %kernel_product.1 = (bf16[4,2048,512]{2,1,0:T(8,128)(2,1)S(1)}, bf16[4,2048,512]{2,1,0:T(8,128)(2,1)S(1)}) custom-call(s32[1]{0:T(128)} %bitcast.2.core_ref, s32[16,16]{1,0:T(8,128)} %table_ref.1, s32[16]{0:T(128)} %occ_ref.1, f32[16,2048]{1,0:T(8,128)} %weight_ref.1, bf16[2048,2048]{1,0:T(8,128)(2,1)} %refs_1_.1, bf16[2048,2048]{1,0:T(8,128)(2,1)} %refs_1_.1, ...), custom_call_target="tpu_custom_call" | custom-call | flops 7000000000 | bytes 8388608 | tf_op jit(solution)/shard_map/kernel_product/pallas_call | solution.py:156
  28.4 0.0 collective-permute-done.refs_3_
  28.4 0.5 collective-permute-start.11
  28.9 0.0 collective-permute-done.10.refs_6_
  28.9 0.0 collective-permute-done.9.refs_5_
  28.9 1.0 %collective-permute-done.11.refs_7_ = f32[16,2048]{1,0:T(8,128)S(1)} collective-permute-done((f32[16,2048]{1,0:T(8,128)S(1)}, f32[16,2048]{1,0:T(8,128)S(1)}, u32[]{:S(2)}, u32[]{:S(2)}) %collective-permute-start.11) | collective-permute-done | bytes 131104 | tf_op jit(solution)/shard_map/ppermute | solution.py:62
  29.9 3.7 %apply_orbitals.1 = f32[8,8,2,8,128]{4,3,2,1,0:T(8,128)S(1)} custom-call(bf16[4,2048,512]{2,1,0:T(8,128)(2,1)S(1)} %get-tuple-element.12.high_ref, bf16[4,2048,512]{2,1,0:T(8,128)(2,1)S(1)} %get-tuple-element.13.low_ref, f32[16,2048]{1,0:T(8,128)S(1)} %collective-permute-done.1.refs_2_.refs_0_, f32[16,2048]{1,0:T(8,128)S(1)} %collective-permute-done.7.refs_1_, ...), custom_call_target="tpu_custom_call" | custom-call | flops 4000000000 | bytes 18874368 | tf_op jit(solution)/shard_map/apply_orbitals/pallas_call | solution.py:202
  33.6 19.7 %all_to_all.5.in_ref = f32[64,2,8,128]{3,2,1,0:T(8,128)S(1)} all-to-all(f32[64,2,8,128]{3,2,1,0:T(8,128)S(1)} %bitcast.4), channel_id=1, replica_groups=mesh['i'=8,'core'=2,'band'=8] {'i','band'}, dimensions={0} | all-to-all | bytes 1048576 | tf_op jit(solution)/shard_map/all_to_all | solution.py:245
  53.3 0.7 %total.1 = f32[16,8,2,128]{3,2,1,0:T(2,128)} custom-call(f32[64,2,8,128]{3,2,1,0:T(8,128)S(1)} %all_to_all.5.in_ref), custom_call_target="tpu_custom_call" | custom-call | tf_op jit(solution)/shard_map/total/pallas_call | solution.py:223
Async XLA Ops:
  1.2 12.7 %collective-permute-start.4 = (f32[16,2048]{1,0:T(8,128)S(1)}, f32[16,2048]{1,0:T(8,128)S(1)}, u32[]{:S(2)}, u32[]{:S(2)}) collective-permute-start(f32[16,2048]{1,0:T(8,128)S(1)} %pick_points.1), channel_id=1, source_target_pairs={{0,1},{1,16},{2,3},{3,18},{4,5},{5,20},{6,7},{7,22},{8,25},{9,24},... | collective-permute-start | bytes 393224 | tf_op jit(solution)/shard_map/ppermute | solution.py:62
  3.0 12.1 %collective-permute-start.3 = (f32[16,2048]{1,0:T(8,128)S(1)}, f32[16,2048]{1,0:T(8,128)S(1)}, u32[]{:S(2)}, u32[]{:S(2)}) collective-permute-start(f32[16,2048]{1,0:T(8,128)S(1)} %pick_points.1), channel_id=1, source_target_pairs={{0,16},{1,1},{2,18},{3,3},{4,20},{5,5},{6,22},{7,7},{8,24},{9,25},... | collective-permute-start | bytes 393224 | tf_op jit(solution)/shard_map/ppermute | solution.py:62
  6.4 8.8 %collective-permute-start.1 = (f32[16,2048]{1,0:T(8,128)S(1)}, f32[16,2048]{1,0:T(8,128)S(1)}, u32[]{:S(2)}, u32[]{:S(2)}) collective-permute-start(f32[16,2048]{1,0:T(8,128)S(1)} %pick_points.1), channel_id=1, source_target_pairs={{0,0},{1,8},{2,2},{3,10},{4,4},{5,12},{6,6},{7,14},{8,1},{9,9},{10... | collective-permute-start | bytes 393224 | tf_op jit(solution)/shard_map/ppermute | solution.py:62
  7.0 11.7 %collective-permute-start.8 = (f32[16,2048]{1,0:T(8,128)S(1)}, f32[16,2048]{1,0:T(8,128)S(1)}, u32[]{:S(2)}, u32[]{:S(2)}) collective-permute-start(f32[16,2048]{1,0:T(8,128)S(1)} %pick_points.1), channel_id=1, source_target_pairs={{0,4},{1,12},{2,6},{3,14},{4,0},{5,8},{6,2},{7,10},{8,5},{9,13},{1... | collective-permute-start | bytes 393224 | tf_op jit(solution)/shard_map/ppermute | solution.py:62
  11.0 9.9 %collective-permute-start.7 = (f32[16,2048]{1,0:T(8,128)S(1)}, f32[16,2048]{1,0:T(8,128)S(1)}, u32[]{:S(2)}, u32[]{:S(2)}) collective-permute-start(f32[16,2048]{1,0:T(8,128)S(1)} %pick_points.1), channel_id=1, source_target_pairs={{0,2},{1,10},{2,0},{3,8},{4,6},{5,14},{6,4},{7,12},{8,3},{9,11},{1... | collective-permute-start | bytes 393224 | tf_op jit(solution)/shard_map/ppermute | solution.py:62
  13.9 8.1 %collective-permute-start.6 = (f32[16,2048]{1,0:T(8,128)S(1)}, f32[16,2048]{1,0:T(8,128)S(1)}, u32[]{:S(2)}, u32[]{:S(2)}) collective-permute-start(f32[16,2048]{1,0:T(8,128)S(1)} %collective-permute-done.4.refs_5_), channel_id=1, source_target_pairs={{0,8},{1,9},{2,10},{3,11},{4,12},{5,13},{6,14},{7,15},{8,0},{9,1},... | collective-permute-start | bytes 393224 | tf_op jit(solution)/shard_map/ppermute | solution.py:62
  15.1 7.0 %collective-permute-start.5 = (f32[16,2048]{1,0:T(8,128)S(1)}, f32[16,2048]{1,0:T(8,128)S(1)}, u32[]{:S(2)}, u32[]{:S(2)}) collective-permute-start(f32[16,2048]{1,0:T(8,128)S(1)} %collective-permute-done.3.refs_4_), channel_id=1, source_target_pairs={{0,8},{1,9},{2,10},{3,11},{4,12},{5,13},{6,14},{7,15},{8,0},{9,1},... | collective-permute-start | bytes 393224 | tf_op jit(solution)/shard_map/ppermute | solution.py:62
  15.2 6.9 %collective-permute-start.2 = (f32[16,2048]{1,0:T(8,128)S(1)}, f32[16,2048]{1,0:T(8,128)S(1)}, u32[]{:S(2)}, u32[]{:S(2)}) collective-permute-start(f32[16,2048]{1,0:T(8,128)S(1)} %collective-permute-done.1.refs_2_.refs_0_), channel_id=1, source_target_pairs={{0,8},{1,9},{2,10},{3,11},{4,12},{5,13},{6,14},{7,15},{8,0},{9,1},... | collective-permute-start | bytes 393224 | tf_op jit(solution)/shard_map/ppermute | solution.py:62
  18.7 9.7 %collective-permute-start = (f32[16,2048]{1,0:T(8,128)S(1)}, f32[16,2048]{1,0:T(8,128)S(1)}, u32[]{:S(2)}, u32[]{:S(2)}) collective-permute-start(f32[16,2048]{1,0:T(8,128)S(1)} %pick_points.1), channel_id=1, source_target_pairs={{0,6},{1,14},{2,4},{3,12},{4,2},{5,10},{6,0},{7,8},{8,7},{9,15},{1... | collective-permute-start | bytes 393224 | tf_op jit(solution)/shard_map/ppermute | solution.py:62
  20.9 8.0 %collective-permute-start.10 = (f32[16,2048]{1,0:T(8,128)S(1)}, f32[16,2048]{1,0:T(8,128)S(1)}, u32[]{:S(2)}, u32[]{:S(2)}) collective-permute-start(f32[16,2048]{1,0:T(8,128)S(1)} %collective-permute-done.8.refs_2_), channel_id=1, source_target_pairs={{0,8},{1,9},{2,10},{3,11},{4,12},{5,13},{6,14},{7,15},{8,0},{9,1},... | collective-permute-start | bytes 393224 | tf_op jit(solution)/shard_map/ppermute | solution.py:62
  22.0 6.9 %collective-permute-start.9 = (f32[16,2048]{1,0:T(8,128)S(1)}, f32[16,2048]{1,0:T(8,128)S(1)}, u32[]{:S(2)}, u32[]{:S(2)}) collective-permute-start(f32[16,2048]{1,0:T(8,128)S(1)} %collective-permute-done.7.refs_1_), channel_id=1, source_target_pairs={{0,8},{1,9},{2,10},{3,11},{4,12},{5,13},{6,14},{7,15},{8,0},{9,1},... | collective-permute-start | bytes 393224 | tf_op jit(solution)/shard_map/ppermute | solution.py:62
  28.4 1.5 %collective-permute-start.11 = (f32[16,2048]{1,0:T(8,128)S(1)}, f32[16,2048]{1,0:T(8,128)S(1)}, u32[]{:S(2)}, u32[]{:S(2)}) collective-permute-start(f32[16,2048]{1,0:T(8,128)S(1)} %collective-permute-done.refs_3_), channel_id=1, source_target_pairs={{0,8},{1,9},{2,10},{3,11},{4,12},{5,13},{6,14},{7,15},{8,0},{9,1},... | collective-permute-start | bytes 393224 | tf_op jit(solution)/shard_map/ppermute | solution.py:62
